TPU v7x, 128 devices: a whole 4x4x4 slice. The times are simulated.
128 devices in a mesh: rep: 16 (over z_lo, x, core), grp: 8 (over z_hi, y).
Axes of the slice: x: 4, y: 4, z: 4 (z_hi: 2, z_lo: 2; z = z_hi * 2 + z_lo), core: 2. Of those that a mesh axis runs over, the one named last changes fastest.
Arguments:
- tokens: bfloat16 [32, 1024, 1024], P('rep', 'grp'), may hold values from -6 to 6
- segments: int32 [32, 1024], P('rep'), may hold values from 0 to 2, as said below
- routes: int32 [32, 1024, 2], P('rep', 'grp'), may hold values from 0 to 5, all different within a row
- cotangent: bfloat16 [32, 1024, 1024], P('rep', 'grp'), may hold values from -6 to 6
- w_qkv: float32 [1024, 2048], P('grp'), may hold values from -0.1875 to 0.1875
- w_out: float32 [1024, 1024], P('grp'), may hold values from -1.5 to 1.5
- w_gateup: float32 [6, 1024, 1024], P(None, 'grp'), may hold values from -0.1875 to 0.1875
- w_down: float32 [6, 512, 1024], P(None, None, 'grp'), may hold values from -0.5 to 0.5
- w_router: float32 [1024, 6], P('grp'), may hold values from -0.09375 to 0.09375
- w_gains: float32 [2, 1024], P(None, 'grp'), may hold values from 0.5 to 1.5
- qkv_first: float32 [1024, 2048], P('grp'), may hold values from -192 to 192
- qkv_second: float32 [1024, 2048], P('grp'), may hold values from 1966.08 to 15400.96
- out_first: float32 [1024, 1024], P('grp'), may hold values from -20 to 20
- out_second: float32 [1024, 1024], P('grp'), may hold values from 19.6608 to 154.0096
- gateup_first: float32 [6, 1024, 1024], P(None, 'grp'), may hold values from -48 to 48
- gateup_second: float32 [6, 1024, 1024], P(None, 'grp'), may hold values from 137.6256 to 1114.112
- down_first: float32 [6, 512, 1024], P(None, None, 'grp'), may hold values from -20 to 20
- down_second: float32 [6, 512, 1024], P(None, None, 'grp'), may hold values from 19.6608 to 154.0096
- router_first: float32 [1024, 6], P('grp'), may hold values from -1280 to 1280
- router_second: float32 [1024, 6], P('grp'), may hold values from 107374.18 to 872415.25
- gains_first: float32 [2, 1024], P(None, 'grp'), may hold values from -192 to 192
- gains_second: float32 [2, 1024], P(None, 'grp'), may hold values from 1966.08 to 15400.96
Outputs:
- layer_out: bfloat16 [32, 1024, 1024], P('rep', 'grp')
- input_grad: float32 [32, 1024, 1024], P('rep', 'grp')
- qkv_moment: float32 [1024, 2048], P('grp')
- qkv_square: float32 [1024, 2048], P('grp')
- qkv_updated: float32 [1024, 2048], P('grp')
- out_moment: float32 [1024, 1024], P('grp')
- out_square: float32 [1024, 1024], P('grp')
- out_updated: float32 [1024, 1024], P('grp')
- gateup_moment: float32 [6, 1024, 1024], P(None, 'grp')
- gateup_square: float32 [6, 1024, 1024], P(None, 'grp')
- gateup_updated: float32 [6, 1024, 1024], P(None, 'grp')
- down_moment: float32 [6, 512, 1024], P(None, None, 'grp')
- down_square: float32 [6, 512, 1024], P(None, None, 'grp')
- down_updated: float32 [6, 512, 1024], P(None, None, 'grp')
- router_moment: float32 [1024, 6], P('grp')
- router_square: float32 [1024, 6], P('grp')
- router_updated: float32 [1024, 6], P('grp')
- gains_moment: float32 [2, 1024], P(None, 'grp')
- gains_square: float32 [2, 1024], P(None, 'grp')
- gains_updated: float32 [2, 1024], P(None, 'grp')
Inputs may be any that keep to these rules, and one draw needn't show every extreme that they name: `routes`: each token names 2 different experts. `segments`: a sequence's segment numbers start at 0 and never fall; of each 2 consecutive sequences one is a single document.
All inputs are finite; a program needn't handle non-finite values.
Results may differ from a plain program's by a relative error of at most 0.034.
Values may be sent and summed in bfloat16 or wider, within the bound.
A program may use at most 256 MiB of HBM per device.

v0:
```python
import jax
import jax.numpy as jnp
from jax import lax
from jax.sharding import PartitionSpec as P

D = 1024
HQ = 16
HK = 8
HD = 64
FF = 512
EXPERTS = 6
TOPK = 2
STEP = 10


beta_one = 0.9
beta_two = 0.95
adam_epsilon = 1e-08
norm_epsilon = 1e-06


def normed(values, gain_vec):
    return (
        values
        * lax.rsqrt(jnp.mean(values * values, axis=-1, keepdims=True) + norm_epsilon)
        * gain_vec
    )


def rotary_tables(positions, head_width):
    freqs = 10000.0 ** (-jnp.arange(head_width // 2).astype(jnp.float32) * 2.0 / head_width)
    angles = positions.astype(jnp.float32)[:, None] * freqs[None, :]
    return (jnp.cos(angles), jnp.sin(angles))


def rotate(tensor, cosine, sine_part):
    half_width = tensor.shape[-1] // 2
    front_half = tensor[..., :half_width]
    back_half = tensor[..., half_width:]
    return jnp.concatenate(
        [front_half * cosine - back_half * sine_part, back_half * cosine + front_half * sine_part],
        axis=-1,
    )


def rotate_back(tensor, cosine, sine_part):
    half_width = tensor.shape[-1] // 2
    front_half = tensor[..., :half_width]
    back_half = tensor[..., half_width:]
    return jnp.concatenate(
        [front_half * cosine + back_half * sine_part, back_half * cosine - front_half * sine_part],
        axis=-1,
    )


def learning_rates():
    return (D ** (-0.5), 8.0 * D ** (-0.5), D ** (-0.5), 2.0 * FF ** (-0.5), 0.5 * D ** (-0.5), 0.5)


def adamw(weight, gradient, moment, square, step_rate, decay_rate):
    moment_new = beta_one * moment + (1.0 - beta_one) * gradient
    square_new = beta_two * square + (1.0 - beta_two) * gradient * gradient
    corrected = moment_new / (1.0 - beta_one**STEP)
    spread = jnp.sqrt(square_new / (1.0 - beta_two**STEP)) + adam_epsilon
    updated = weight - step_rate * (corrected / spread + decay_rate * weight)
    return [moment_new, square_new, updated]


def on_device(
    tokens,
    segments,
    routes,
    cotangent,
    w_qkv,
    w_out,
    w_gateup,
    w_down,
    w_router,
    w_gains,
    qkv_first,
    qkv_second,
    out_first,
    out_second,
    gateup_first,
    gateup_second,
    down_first,
    down_second,
    router_first,
    router_second,
    gains_first,
    gains_second,
):
    member = lax.axis_index("grp")
    seq_count, span_rows, model_width = tokens.shape
    seq_length = segments.shape[1]
    row_count = seq_count * span_rows
    group_ratio = HQ // HK
    query_width = HQ * HD
    key_width = HK * HD
    scaling = HD ** (-0.5)
    f32 = jnp.float32
    b16 = jnp.bfloat16
    gathered = (
        lax.all_gather(w_qkv.astype(b16), "grp", axis=0, tiled=True),
        lax.all_gather(w_out.astype(b16), "grp", axis=0, tiled=True),
        lax.all_gather(w_gateup.astype(b16), "grp", axis=1, tiled=True),
        lax.all_gather(w_down.astype(b16), "grp", axis=2, tiled=True),
        lax.all_gather(w_router.astype(b16), "grp", axis=0, tiled=True),
        lax.all_gather(w_gains.astype(b16), "grp", axis=1, tiled=True),
    )
    wqkv_low, wout_low, wgateup_low, wdown_low, wrouter_low, wgains_low = gathered
    gain_one = wgains_low[0].astype(f32)
    gain_two = wgains_low[1].astype(f32)
    inputs = tokens.reshape(row_count, model_width).astype(f32)
    act_one = normed(inputs, gain_one).astype(b16)
    projected = jnp.dot(act_one, wqkv_low, preferred_element_type=f32)
    positions = member * span_rows + jnp.arange(span_rows)
    cosine, sine_part = rotary_tables(positions, HD)
    cosine = cosine[:, None, :]
    sine_part = sine_part[:, None, :]
    queries = rotate(
        projected[:, :query_width].reshape(seq_count, span_rows, HQ, HD), cosine, sine_part
    ).astype(b16)
    key_local = rotate(
        projected[:, query_width : query_width + key_width].reshape(seq_count, span_rows, HK, HD),
        cosine,
        sine_part,
    ).astype(b16)
    value_local = (
        projected[:, query_width + key_width :].reshape(seq_count, span_rows, key_width).astype(b16)
    )
    all_keys, all_values = (
        lax.all_gather(
            key_local.reshape(seq_count, span_rows, key_width), "grp", axis=1, tiled=True
        ),
        lax.all_gather(value_local, "grp", axis=1, tiled=True),
    )
    all_keys = all_keys.reshape(seq_count, seq_length, HK, HD)
    all_values = all_values.reshape(seq_count, seq_length, HK, HD)
    queries = queries.reshape(seq_count, span_rows, HK, group_ratio, HD)
    own_segments = lax.dynamic_slice_in_dim(segments, member * span_rows, span_rows, 1)
    causal = positions[:, None] >= jnp.arange(seq_length)[None, :]
    allowed = causal[None] & (own_segments[:, :, None] == segments[:, None, :])
    allowed = allowed[:, None, None]

    def scores_of():
        raw_scores = jnp.einsum("bqhgd,bkhd->bhgqk", queries, all_keys, preferred_element_type=f32)
        return jnp.where(allowed, raw_scores * scaling, -1e30)

    scores = scores_of()
    highest = jnp.max(scores, axis=-1, keepdims=True)
    powers = jnp.exp(scores - highest)
    summed_exp = jnp.sum(powers, axis=-1, keepdims=True)
    probs_low = (powers / summed_exp).astype(b16)
    log_total = highest + jnp.log(summed_exp)
    heads_out = (
        jnp.einsum("bhgqk,bkhd->bqhgd", probs_low, all_values, preferred_element_type=f32)
        .reshape(row_count, query_width)
        .astype(b16)
    )
    hidden = inputs + jnp.dot(heads_out, wout_low, preferred_element_type=f32)
    act_two = normed(hidden, gain_two).astype(b16)
    logits = jnp.dot(act_two, wrouter_low, preferred_element_type=f32)
    route_ids = routes.reshape(row_count, TOPK)
    chosen = (route_ids[:, :, None] == jnp.arange(EXPERTS)[None, None, :]).astype(f32)
    picked = jnp.sum(chosen * logits[:, None, :], axis=-1)
    pick_top = jnp.max(picked, axis=-1, keepdims=True)
    pick_powers = jnp.exp(picked - pick_top)
    gate_probs = pick_powers / jnp.sum(pick_powers, axis=-1, keepdims=True)
    mixing = jnp.sum(gate_probs[:, :, None] * chosen, axis=1)
    gate_up = jnp.einsum("rd,edf->ref", act_two, wgateup_low, preferred_element_type=f32)
    gate_part = gate_up[..., :FF]
    up_part = gate_up[..., FF:]
    sigmoid_gate = jax.nn.sigmoid(gate_part)
    silu_gate = gate_part * sigmoid_gate
    inner = (silu_gate * up_part).astype(b16)
    expert_out = jnp.einsum("ref,efd->red", inner, wdown_low, preferred_element_type=f32)
    result = hidden + jnp.sum(mixing[:, :, None] * expert_out, axis=1)
    layer_out = result.astype(b16).reshape(seq_count, span_rows, model_width)
    grad_out = cotangent.reshape(row_count, model_width).astype(f32)
    grad_expert = (mixing[:, :, None] * grad_out[:, None, :]).astype(b16)
    grad_mixing = jnp.sum(expert_out * grad_out[:, None, :], axis=-1)
    grad_inner = jnp.einsum("red,efd->ref", grad_expert, wdown_low, preferred_element_type=f32)
    down_grad = jnp.einsum("ref,red->efd", inner, grad_expert, preferred_element_type=f32)
    silu_slope = sigmoid_gate * (1.0 + gate_part * (1.0 - sigmoid_gate))
    grad_gate_up = jnp.concatenate(
        [grad_inner * up_part * silu_slope, grad_inner * silu_gate], axis=-1
    ).astype(b16)
    grad_act_two = jnp.einsum("ref,edf->rd", grad_gate_up, wgateup_low, preferred_element_type=f32)
    gateup_grad = jnp.einsum("rd,ref->edf", act_two, grad_gate_up, preferred_element_type=f32)
    grad_gates = jnp.sum(chosen * grad_mixing[:, None, :], axis=-1)
    grad_picked = gate_probs * (
        grad_gates - jnp.sum(gate_probs * grad_gates, axis=-1, keepdims=True)
    )
    grad_logits = jnp.sum(chosen * grad_picked[:, :, None], axis=1).astype(b16)
    grad_act_two = grad_act_two + jnp.einsum(
        "re,de->rd", grad_logits, wrouter_low, preferred_element_type=f32
    )
    router_grad = jnp.einsum("rd,re->de", act_two, grad_logits, preferred_element_type=f32)
    norm_unused, second_pull = jax.vjp(normed, hidden, gain_two)
    grad_hidden, gain_two_grad = second_pull(grad_act_two)
    grad_hidden = grad_hidden + grad_out
    grad_heads = grad_hidden.astype(b16)
    out_grad = jnp.einsum("rh,rd->hd", heads_out, grad_heads, preferred_element_type=f32)
    grad_heads_in = jnp.einsum(
        "rd,hd->rh", grad_heads, wout_low, preferred_element_type=f32
    ).astype(b16)
    grad_heads_in = grad_heads_in.reshape(seq_count, span_rows, HK, group_ratio, HD)
    scores = scores_of()
    probs_full = jnp.exp(scores - log_total)
    probs_again = probs_full.astype(b16)
    grad_probs = jnp.einsum(
        "bqhgd,bkhd->bhgqk", grad_heads_in, all_values, preferred_element_type=f32
    )
    value_grad = jnp.einsum(
        "bhgqk,bqhgd->bkhd", probs_again, grad_heads_in, preferred_element_type=f32
    )
    grad_scores = probs_full * (
        grad_probs - jnp.sum(probs_full * grad_probs, axis=-1, keepdims=True)
    )
    grad_raw = jnp.where(allowed, grad_scores * scaling, 0.0).astype(b16)
    query_grad = jnp.einsum("bhgqk,bkhd->bqhgd", grad_raw, all_keys, preferred_element_type=f32)
    key_grad = jnp.einsum("bhgqk,bqhgd->bkhd", grad_raw, queries, preferred_element_type=f32)
    key_grad, value_grad = (
        lax.psum_scatter(
            key_grad.reshape(seq_count, seq_length, key_width).astype(jnp.bfloat16),
            "grp",
            scatter_dimension=1,
            tiled=True,
        ).astype(jnp.float32),
        lax.psum_scatter(
            value_grad.reshape(seq_count, seq_length, key_width).astype(jnp.bfloat16),
            "grp",
            scatter_dimension=1,
            tiled=True,
        ).astype(jnp.float32),
    )
    query_grad = rotate_back(query_grad.reshape(seq_count, span_rows, HQ, HD), cosine, sine_part)
    key_grad = rotate_back(key_grad.reshape(seq_count, span_rows, HK, HD), cosine, sine_part)
    grad_projected = jnp.concatenate(
        [
            query_grad.reshape(row_count, query_width),
            key_grad.reshape(row_count, key_width),
            value_grad.reshape(row_count, key_width),
        ],
        axis=-1,
    ).astype(b16)
    grad_act_one = jnp.einsum("rf,df->rd", grad_projected, wqkv_low, preferred_element_type=f32)
    qkv_grad = jnp.einsum("rd,rf->df", act_one, grad_projected, preferred_element_type=f32)
    first_unused, first_pull = jax.vjp(normed, inputs, gain_one)
    grad_inputs, gain_one_grad = first_pull(grad_act_one)
    input_grad = (grad_inputs + grad_hidden).reshape(seq_count, span_rows, model_width)
    gains_grad = jnp.stack([gain_one_grad, gain_two_grad])
    masters = (w_qkv, w_out, w_gateup, w_down, w_router, w_gains)
    first_moments = (qkv_first, out_first, gateup_first, down_first, router_first, gains_first)
    second_moments = (
        qkv_second,
        out_second,
        gateup_second,
        down_second,
        router_second,
        gains_second,
    )
    step_rates = learning_rates()
    decay_rates = (0.1, 0.1, 0.1, 0.1, 0.1, 0.0)
    summed = (
        lax.psum_scatter(
            qkv_grad.astype(jnp.bfloat16), "grp", scatter_dimension=0, tiled=True
        ).astype(jnp.float32),
        lax.psum_scatter(
            out_grad.astype(jnp.bfloat16), "grp", scatter_dimension=0, tiled=True
        ).astype(jnp.float32),
        lax.psum_scatter(
            gateup_grad.astype(jnp.bfloat16), "grp", scatter_dimension=1, tiled=True
        ).astype(jnp.float32),
        lax.psum_scatter(
            down_grad.astype(jnp.bfloat16), "grp", scatter_dimension=2, tiled=True
        ).astype(jnp.float32),
        lax.psum_scatter(
            router_grad.astype(jnp.bfloat16), "grp", scatter_dimension=0, tiled=True
        ).astype(jnp.float32),
        lax.psum_scatter(
            gains_grad.astype(jnp.bfloat16), "grp", scatter_dimension=1, tiled=True
        ).astype(jnp.float32),
    )
    summed = (
        lax.psum(summed[0].astype(jnp.bfloat16), "rep").astype(jnp.float32),
        lax.psum(summed[1].astype(jnp.bfloat16), "rep").astype(jnp.float32),
        lax.psum(summed[2].astype(jnp.bfloat16), "rep").astype(jnp.float32),
        lax.psum(summed[3].astype(jnp.bfloat16), "rep").astype(jnp.float32),
        lax.psum(summed[4].astype(jnp.bfloat16), "rep").astype(jnp.float32),
        lax.psum(summed[5].astype(jnp.bfloat16), "rep").astype(jnp.float32),
    )
    results = []
    for slot_index in range(6):
        results = results + adamw(
            masters[slot_index],
            summed[slot_index],
            first_moments[slot_index],
            second_moments[slot_index],
            step_rates[slot_index],
            decay_rates[slot_index],
        )
    return (
        layer_out,
        input_grad,
        results[0],
        results[1],
        results[2],
        results[3],
        results[4],
        results[5],
        results[6],
        results[7],
        results[8],
        results[9],
        results[10],
        results[11],
        results[12],
        results[13],
        results[14],
        results[15],
        results[16],
        results[17],
    )


def solution(mesh):
    return jax.shard_map(
        on_device,
        mesh=mesh,
        in_specs=(
            P("rep", "grp", None),
            P("rep", None),
            P("rep", "grp", None),
            P("rep", "grp", None),
            P("grp", None),
            P("grp", None),
            P(None, "grp", None),
            P(None, None, "grp"),
            P("grp", None),
            P(None, "grp"),
            P("grp", None),
            P("grp", None),
            P("grp", None),
            P("grp", None),
            P(None, "grp", None),
            P(None, "grp", None),
            P(None, None, "grp"),
            P(None, None, "grp"),
            P("grp", None),
            P("grp", None),
            P(None, "grp"),
            P(None, "grp"),
        ),
        out_specs=(
            P("rep", "grp", None),
            P("rep", "grp", None),
            P("grp", None),
            P("grp", None),
            P("grp", None),
            P("grp", None),
            P("grp", None),
            P("grp", None),
            P(None, "grp", None),
            P(None, "grp", None),
            P(None, "grp", None),
            P(None, None, "grp"),
            P(None, None, "grp"),
            P(None, None, "grp"),
            P("grp", None),
            P("grp", None),
            P("grp", None),
            P(None, "grp"),
            P(None, "grp"),
            P(None, "grp"),
        ),
        check_vma=False,
    )
```

profile of v0, /device:TPU:1, one launch (start us, length us, event | category | flops | bytes accessed | tf_op | source)
XLA Modules:
  0.0 1461.3 jit_solution(3599621364981531788)
XLA Ops:
  10.1 21.4 %all_gather.24 = bf16[2,1024]{1,0:T(2,128)(2,1)S(1)} all-gather(bf16[2,128]{1,0:T(2,128)(2,1)S(1)} %convert_element_type.183), channel_id=1, replica_groups=mesh['rep'=16,'grp'=8] {'grp'}, dimensions={1}, use_global_device_ids=true | all-gather | bytes 4608 | tf_op jit(solution)/shard_map/all_gather | solution.py:109
  34.5 50.9 %all-gather.7.cloned.1.call-done = bf16[1024,2048]{1,0:T(8,128)(2,1)} async-done(((bf16[128,2048]{1,0:T(8,128)(2,1)}), bf16[1024,2048]{1,0:T(8,128)(2,1)}) %all-gather.7.cloned.1.call-update) | async-done | bytes 4194320 | tf_op jit(solution)/shard_map/all_gather | solution.py:104
  106.9 25.9 %all_gather.29 = bf16[1024,6]{0,1:T(8,128)(2,1)S(1)} all-gather(bf16[128,6]{0,1:T(8,128)(2,1)S(1)} %convert_element_type.196), channel_id=1, replica_groups=mesh['rep'=16,'grp'=8] {'grp'}, dimensions={0}, use_global_device_ids=true | all-gather | bytes 13824 | tf_op jit(solution)/shard_map/all_gather | solution.py:108
  145.9 56.5 %all-gather.11.cloned.1.call-done = bf16[2,1024,512]{1,2,0:T(8,128)(2,1)} async-done(((bf16[2,128,512]{1,2,0:T(8,128)(2,1)}), bf16[2,1024,512]{1,2,0:T(8,128)(2,1)}) %all-gather.11.cloned.1.call-update) | async-done | bytes 2097168 | tf_op jit(solution)/shard_map/all_gather | solution.py:133
  202.4 10.0 fusion.93
  229.1 29.4 %all-gather.13.cloned.1.call-done = bf16[1024,1024]{1,0:T(8,128)(2,1)} async-done(((bf16[128,1024]{1,0:T(8,128)(2,1)}), bf16[1024,1024]{1,0:T(8,128)(2,1)}) %all-gather.13.cloned.1.call-update) | async-done | bytes 2097168 | tf_op jit(solution)/shard_map/all_gather | solution.py:105
  261.5 146.8 %all-gather.15.cloned.1.call-done = bf16[6,1024,1024]{2,1,0:T(8,128)(2,1)} async-done(((bf16[6,128,1024]{2,1,0:T(8,128)(2,1)}), bf16[6,1024,1024]{2,1,0:T(8,128)(2,1)}) %all-gather.15.cloned.1.call-update) | async-done | bytes 12582928 | tf_op jit(solution)/shard_map/all_gather | solution.py:106
  408.3 10.0 fusion.52
  418.3 89.3 %all-gather.17.cloned.1.call-done = bf16[6,512,1024]{2,1,0:T(8,128)(2,1)} async-done(((bf16[6,512,128]{2,1,0:T(8,128)(2,1)}), bf16[6,512,1024]{2,1,0:T(8,128)(2,1)}) %all-gather.17.cloned.1.call-update) | async-done | bytes 6291472 | tf_op jit(solution)/shard_map/all_gather | solution.py:107
  546.3 24.1 %bitcast_convert_fusion.1 = bf16[2,8,64,1024]{3,2,1,0:T(8,128)(2,1)} fusion(f32[2,8,1024,128,2]{3,2,4,1,0:T(8,128)} %fusion.96, f32[2,8,2,128,1024]{3,4,2,1,0:T(8,128)} %get-tuple-element.152, f32[2,8,2,128]{3,2,1,0:T(2,128)S(1)} %bitcast.233, pred[2,128,1024]{1,2,0:T(8,128)(4,1)S(1)} %compare_and_fusion, bf16[2,128,8,2,32]{1,4,3,2,0:T(8,128)(2,1)} %bitcast.217, ...), kind=kOutput, calls=%fused_computation.29 | convolution fusion | flops 572527616 | bytes 36454400 | tf_op jit(solution)/shard_map/bhgqk,bqhgd->bkhd/dot_general | solution.py:223
  595.6 12.5 copy.171
  608.1 10.3 copy.188
  627.8 23.1 %copy.169 = bf16[6,1024,1024]{2,0,1:T(8,128)(2,1)} copy(bf16[6,1024,1024]{1,2,0:T(8,128)(2,1)} %convert_bitcast_fusion) | data formatting | bytes 25165824
  650.9 14.6 %copy.187 = bf16[128,8,6,1024]{3,1,2,0:T(8,128)(2,1)} copy(bf16[128,8,6,1024]{3,2,1,0:T(8,128)(2,1)} %bitcast.192) | data formatting | bytes 25165824
  668.7 24.0 %fusion.15 = f32[2,8,64,2,128]{4,2,3,1,0:T(8,128)S(1)} fusion(bf16[2,1024,8,64,1]{1,3,4,2,0:T(8,128)(2,1)} %bitcast.213, f32[2,8,1024,128,2]{3,2,4,1,0:T(8,128)} %fusion.96, f32[2,8,2,128,1024]{3,4,2,1,0:T(8,128)} %get-tuple-element.152, f32[2,8,2,128]{3,2,1,0:T(2,128)S(1)} %bitcast.235, pred[2,128,1024]{1,2,0:T(8,128)(4,1)S(1)} %compare_and_fusion), kind=kOutput, calls=%fused_computation.25 | convolution fusion | flops 570430464 | bytes 36978688 | tf_op jit(solution)/shard_map/bhgqk,bkhd->bqhgd/dot_general | solution.py:222
  696.9 32.7 %reduce-scatter.19.cloned.1.call-done = bf16[2,128,512]{2,1,0:T(8,128)(2,1)} async-done(((bf16[2,1024,512]{2,1,0:T(8,128)(2,1)}), bf16[2,128,512]{2,1,0:T(8,128)(2,1)}) %reduce-scatter.19.cloned.1.call-update) | async-done | bytes 262160 | tf_op jit(solution)/shard_map/reduce_scatter | solution.py:231
  740.8 91.5 %reduce-scatter.29.cloned.1.call-done = bf16[128,3072]{1,0:T(8,128)(2,1)} async-done(((bf16[1024,3072]{1,0:T(8,128)(2,1)}), bf16[128,3072]{1,0:T(8,128)(2,1)}) %reduce-scatter.29.cloned.1.call-update) | async-done | bytes 786448
  836.0 151.1 %reduce-scatter.27.cloned.1.call-done = bf16[128,6144]{1,0:T(8,128)(2,1)} async-done(((bf16[1024,6144]{1,0:T(8,128)(2,1)}), bf16[128,6144]{1,0:T(8,128)(2,1)}) %reduce-scatter.27.cloned.1.call-update) | async-done | bytes 1572880
  993.2 70.5 %reduce-scatter.23.cloned.1.call-done = bf16[128,1024]{1,0:T(8,128)(2,1)} async-done(((bf16[1024,1024]{1,0:T(8,128)(2,1)}), bf16[128,1024]{1,0:T(8,128)(2,1)}) %reduce-scatter.23.cloned.1.call-update) | async-done | bytes 262160 | tf_op jit(solution)/shard_map/reduce_scatter | solution.py:270
  1063.6 87.9 %reduce-scatter.21.cloned.1.call-done = bf16[128,2048]{1,0:T(8,128)(2,1)} async-done(((bf16[1024,2048]{1,0:T(8,128)(2,1)}), bf16[128,2048]{1,0:T(8,128)(2,1)}) %reduce-scatter.21.cloned.1.call-update) | async-done | bytes 524304 | tf_op jit(solution)/shard_map/reduce_scatter | solution.py:267
  1162.4 62.0 %reduce-scatter.31.cloned.1.call-done = bf16[128,6]{1,0:T(8,128)(2,1)} async-done(((bf16[1024,6]{1,0:T(8,128)(2,1)}), bf16[128,6]{1,0:T(8,128)(2,1)}) %reduce-scatter.31.cloned.1.call-update) | async-done | bytes 1552
  1226.5 71.0 %reduce-scatter.33.cloned.1.call-done = bf16[128,2]{1,0:T(8,128)(2,1)} async-done(((bf16[1024,2]{1,0:T(8,128)(2,1)}), bf16[128,2]{1,0:T(8,128)(2,1)}) %reduce-scatter.33.cloned.1.call-update) | async-done | bytes 528
  1298.4 29.1 %all-reduce = (bf16[128,6]{0,1:T(8,128)(2,1)S(1)}, bf16[2,128]{1,0:T(2,128)(2,1)S(1)}) all-reduce(bf16[128,6]{0,1:T(8,128)(2,1)S(1)} %copy.174, bf16[2,128]{1,0:T(2,128)(2,1)S(1)} %copy.176), channel_id=1, replica_groups=mesh['rep'=16,'grp'=8] {'rep'}, use_global_device_ids=true, to_apply=%region_27.28 | all-reduce | flops 1024 | bytes 4096 | tf_op jit(solution)/shard_map/psum | solution.py:291
  1328.7 99.9 %all-reduce.4.cloned.1.call-done = (bf16[128,2048]{1,0:T(8,128)(2,1)}, bf16[128,1024]{1,0:T(8,128)(2,1)}, bf16[6,128,1024]{1,2,0:T(8,128)(2,1)}, bf16[6,512,128]{2,1,0:T(8,128)(2,1)}) async-done(((bf16[128,2048]{1,0:T(8,128)(2,1)}, bf16[128,1024]{1,0:T(8,128)(2,1)}, bf16[6,128,1024]{1,2,0:T(8,128)(2,1)}, bf16[6,512,128]{2,1,0:T(8,128)(2,1)}), (bf16[128,2048]{1,0:T(8,128)(2,1)}, bf16[128,1024]{1,0:T(8,128)(2,1)}, ...) | async-done | bytes 3145744 | tf_op jit(solution)/shard_map/psum | solution.py:287
  (242 shorter events, 201.7 us)
Async XLA Ops:
  7.2 78.2 %all-gather.7.cloned.1.call-start = ((), (), s32[]{:S(2)}) async-start(), calls=%async_computation.8 | async-start | bytes 4718592 | tf_op jit(solution)/shard_map/all_gather | solution.py:104
  9.3 133.5 %all-gather.9.cloned.1.call-start = ((), (), s32[]{:S(2)}) async-start(), calls=%async_computation.9 | async-start | bytes 2359296 | tf_op jit(solution)/shard_map/all_gather | solution.py:136
  91.0 111.4 %all-gather.11.cloned.1.call-start = ((), (), s32[]{:S(2)}) async-start(), calls=%async_computation.10 | async-start | bytes 2359296 | tf_op jit(solution)/shard_map/all_gather | solution.py:133
  99.8 158.6 %all-gather.13.cloned.1.call-start = ((), (), s32[]{:S(2)}) async-start(), calls=%async_computation.11 | async-start | bytes 2359296 | tf_op jit(solution)/shard_map/all_gather | solution.py:105
  101.7 306.6 %all-gather.15.cloned.1.call-start = ((), (), s32[]{:S(2)}) async-start(), calls=%async_computation.12 | async-start | bytes 14155776 | tf_op jit(solution)/shard_map/all_gather | solution.py:106
  103.2 404.4 %all-gather.17.cloned.1.call-start = ((), (), s32[]{:S(2)}) async-start(), calls=%async_computation.13 | async-start | bytes 7077888 | tf_op jit(solution)/shard_map/all_gather | solution.py:107
  105.8 588.8 %reduce-scatter.25.cloned.1.call-start = ((), (), s32[]{:S(2)}) async-start(), calls=%async_computation.17 | async-start | bytes 2359296
  135.0 77.5 %copy-start.21 = (bf16[2,128,16,32]{1,3,2,0:T(8,128)(2,1)}, bf16[2,128,16,32]{1,3,2,0:T(8,128)(2,1)S(1)}, u32[]{:S(2)}) copy-start(bf16[2,128,16,32]{1,3,2,0:T(8,128)(2,1)S(1)} %copy.132) | copy-start | bytes 786436
  261.1 157.2 %copy-start.9 = (bf16[256,1024]{1,0:T(8,128)(2,1)}, bf16[256,1024]{1,0:T(8,128)(2,1)S(1)}, u32[]{:S(2)}) copy-start(bf16[256,1024]{1,0:T(8,128)(2,1)S(1)} %multiply_convert_fusion.6) | copy-start | bytes 1572868
  261.5 246.1 %copy-start.11 = (f32[256,1024]{1,0:T(8,128)S(1)}, f32[256,1024]{1,0:T(8,128)}, u32[]{:S(2)}) copy-start(f32[256,1024]{1,0:T(8,128)} %convert.68) | copy-start | bytes 3145732
  577.1 152.4 %reduce-scatter.19.cloned.1.call-start = ((), (), s32[]{:S(2)}) async-start(), calls=%async_computation.14 | async-start | bytes 2359296 | tf_op jit(solution)/shard_map/reduce_scatter | solution.py:231
  588.4 243.8 %reduce-scatter.29.cloned.1.call-start = ((), (), s32[]{:S(2)}) async-start(), calls=%async_computation.19 | async-start | bytes 7077888
  618.4 368.6 %reduce-scatter.27.cloned.1.call-start = ((), (), s32[]{:S(2)}) async-start(), calls=%async_computation.18 | async-start | bytes 14155776
  665.5 398.1 %reduce-scatter.23.cloned.1.call-start = ((), (), s32[]{:S(2)}) async-start(), calls=%async_computation.16 | async-start | bytes 2359296 | tf_op jit(solution)/shard_map/reduce_scatter | solution.py:270
  668.6 482.9 %reduce-scatter.21.cloned.1.call-start = ((), (), s32[]{:S(2)}) async-start(), calls=%async_computation.15 | async-start | bytes 4718592 | tf_op jit(solution)/shard_map/reduce_scatter | solution.py:267
  734.0 490.4 %reduce-scatter.31.cloned.1.call-start = ((), (), s32[]{:S(2)}) async-start(), calls=%async_computation.20 | async-start | bytes 294912
  735.1 562.4 %reduce-scatter.33.cloned.1.call-start = ((), (), s32[]{:S(2)}) async-start(), calls=%async_computation.21 | async-start | bytes 294912
  740.7 687.9 %all-reduce.4.cloned.1.call-start = ((), (), s32[]{:S(2)}) async-start(), calls=%async_computation.22 | async-start | bytes 6291456 | tf_op jit(solution)/shard_map/psum | solution.py:287
  1162.3 165.1 %copy-start.46 = (f32[2,128]{1,0:T(2,128)S(1)}, f32[2,128]{1,0:T(2,128)}, u32[]{:S(2)}) copy-start(f32[2,128]{1,0:T(2,128)} %param.31) | copy-start | bytes 3076
  1162.3 165.1 %copy-start.47 = (f32[2,128]{1,0:T(2,128)S(1)}, f32[2,128]{1,0:T(2,128)}, u32[]{:S(2)}) copy-start(f32[2,128]{1,0:T(2,128)} %param.43) | copy-start | bytes 3076
  1162.3 165.1 %copy-start.48 = (f32[2,128]{1,0:T(2,128)S(1)}, f32[2,128]{1,0:T(2,128)}, u32[]{:S(2)}) copy-start(f32[2,128]{1,0:T(2,128)} %param.42) | copy-start | bytes 3076
  1162.3 165.7 %copy-start.38 = (f32[128,6]{0,1:T(8,128)S(1)}, f32[128,6]{0,1:T(8,128)}, u32[]{:S(2)}) copy-start(f32[128,6]{0,1:T(8,128)} %param.30) | copy-start | bytes 9220
  1162.3 165.7 %copy-start.44 = (f32[128,6]{0,1:T(8,128)S(1)}, f32[128,6]{0,1:T(8,128)}, u32[]{:S(2)}) copy-start(f32[128,6]{0,1:T(8,128)} %param.41) | copy-start | bytes 9220
  1162.4 165.7 %copy-start.45 = (f32[128,6]{0,1:T(8,128)S(1)}, f32[128,6]{0,1:T(8,128)}, u32[]{:S(2)}) copy-start(f32[128,6]{0,1:T(8,128)} %param.40) | copy-start | bytes 9220
  (44 other events, 908.3 us)
Sparse Core Ops, SparseCore 0:
  10.9 74.4 all-gather.6
  91.1 51.7 all-gather.8
  145.7 56.7 all-gather.10
  205.2 53.2 all-gather.12
  261.2 146.9 all-gather.14
  410.9 96.6 all-gather.16
  577.3 73.4 reduce-scatter.24
  655.6 73.9 reduce-scatter.18
  733.5 98.7 reduce-scatter.28
  836.5 150.4 reduce-scatter.26
  991.4 72.1 reduce-scatter.22
  1067.9 83.6 reduce-scatter.20
  1156.1 68.2 reduce-scatter.30
  1228.4 69.1 reduce-scatter.32
  1301.5 127.0 all-reduce.3
where the time goes:
time: 1470 us; the launch traced here: 1460 us
  waiting for transfers between devices  1050 us (71%)
  matrix products  144 us (10%)
  local copies, waits for them, and re-layouts  131 us (9%)
  blocking collectives  76.4 us (5%)
  other arithmetic  46.4 us (3%)
  between operations  15.1 us (1%)
    unnamed x20, waiting for transfers between devices  376 us
    all_gather x1, waiting for transfers between devices, on_device(): lax.all_gather(w_gateup.astype(b16), 'grp', axis=1, tiled=True)  147 us
    unnamed x128, local copies, waits for them, and re-layouts  108 us
    psum x1, waiting for transfers between devices, on_device(): lax.psum(summed[0].astype(jnp.bfloat16), 'rep').astype(jnp.float32)  99.9 us
    all_gather x1, waiting for transfers between devices, on_device(): lax.all_gather(w_down.astype(b16), 'grp', axis=2, tiled=True)  89.3 us
    reduce_scatter x1, waiting for transfers between devices, on_device(): lax.psum_scatter(qkv_grad.astype(jnp.bfloat16), 'grp', scatter_dimension=...  87.9 us
    reduce_scatter x1, waiting for transfers between devices, on_device(): lax.psum_scatter(out_grad.astype(jnp.bfloat16), 'grp', scatter_dimension=...  70.5 us
    all_gather x1, waiting for transfers between devices, on_device(): lax.all_gather(key_local.reshape(seq_count, span_rows, key_width), 'grp',...  56.5 us
  transfers between devices with their start and end apart: 15, of which 14 were waited for; matrix products, arithmetic and copies ran while one was open for 15% of the time, Pallas kernels for 0%

commit v1 on v0

v1 whole, which is shorter than its diff:
```python
import functools

import jax
import jax.numpy as jnp
from jax import lax
from jax.experimental import pallas as pl
from jax.experimental.pallas import tpu as pltpu
from jax.sharding import PartitionSpec as P

D = 1024
HQ = 16
HK = 8
HD = 64
FF = 512
EXPERTS = 6
TOPK = 2
STEP = 10
ROWS = 256
SLICE = 64
WIDE = EXPERTS * SLICE

beta_one = 0.9
beta_two = 0.95
adam_epsilon = 1e-08
norm_epsilon = 1e-06

f32 = jnp.float32
b16 = jnp.bfloat16
MESH = pl.DeviceIdType.MESH
ANY = pl.BlockSpec(memory_space=pl.ANY)
VMEM = pl.BlockSpec(memory_space=pltpu.VMEM)
MIB = 2**20


def place():
    rep = lax.axis_index("rep")
    grp = lax.axis_index("grp")
    z_lo, x, c = rep // 8, lax.rem(rep // 2, 4), lax.rem(rep, 2)
    z_hi, y = grp // 4, lax.rem(grp, 4)
    return x, y, z_hi * 2 + z_lo, c


def dev(x, y, z, c):
    x, y, z = lax.rem(x + 4, 4), lax.rem(y + 4, 4), lax.rem(z + 4, 4)
    return (lax.rem(z, 2) * 8 + x * 2 + c, (z // 2) * 4 + y)


class Net:
    def __init__(self, send_sems, recv_sems, local_sems):
        self.sems = (send_sems, recv_sems, local_sems)
        self.count = 0
        self.locals = 0
        self.open = []

    def greet(self, peers):
        bar = pltpu.get_barrier_semaphore()
        for peer in peers:
            pl.semaphore_signal(bar, inc=1, device_id=peer, device_id_type=MESH)
        pl.semaphore_wait(bar, len(peers))

    def send(self, src, dst, peer):
        copy = pltpu.make_async_remote_copy(
            src_ref=src,
            dst_ref=dst,
            send_sem=self.sems[0].at[self.count],
            recv_sem=self.sems[1].at[self.count],
            device_id=peer,
            device_id_type=MESH,
        )
        copy.start()
        self.count += 1
        self.open.append(copy)
        return copy

    def local(self, src, dst):
        copy = pltpu.make_async_copy(src, dst, self.sems[2].at[self.locals])
        copy.start()
        self.locals += 1
        return copy

    def got(self, copy):
        copy.wait_recv()
        copy.seen = True

    def finish(self):
        for copy in self.open:
            if not getattr(copy, "seen", False):
                copy.wait_recv()
            copy.wait_send()


def sems(n, n_local=1):
    return [
        pltpu.SemaphoreType.DMA((n,)),
        pltpu.SemaphoreType.DMA((n,)),
        pltpu.SemaphoreType.DMA((n_local,)),
    ]


def params(cid=None, mib=56):
    if cid is None:
        return pltpu.CompilerParams(vmem_limit_bytes=mib * MIB)
    return pltpu.CompilerParams(
        vmem_limit_bytes=mib * MIB, collective_id=cid, has_side_effects=True
    )


def shape(dims, dtype):
    return jax.ShapeDtypeStruct(dims, dtype)


def ring_gather(net, part, right, left, me, src=None):
    src = src or (lambda half: part(me, half))
    a1 = net.send(src(0), part(me, 0), right)
    b1 = net.send(src(1), part(me, 1), left)
    a2 = net.send(src(1), part(me, 1), right)
    b2 = net.send(src(0), part(me, 0), left)
    before, after = lax.rem(me + 3, 4), lax.rem(me + 1, 4)
    net.got(a1)
    a3 = net.send(part(before, 0), part(before, 0), right)
    net.got(b1)
    b3 = net.send(part(after, 1), part(after, 1), left)
    for copy in (a2, b2, a3, b3):
        net.got(copy)


def add_into(dst, one, two, rows, step):
    def body(i, carry):
        at = pl.ds(pl.multiple_of(i * step, step), step)
        dst[at] = (one[at].astype(f32) + two[at].astype(f32)).astype(b16)
        return carry

    lax.fori_loop(0, rows // step, body, 0)


def ring_scatter(net, part, tmp, got, right, left, me, rows, step):
    half = rows // 2
    lo, hi = pl.ds(0, half), pl.ds(half, half)
    after, before, across = lax.rem(me + 1, 4), lax.rem(me + 3, 4), lax.rem(me + 2, 4)
    s1 = net.send(part(across).at[lo], tmp.at[0], right)
    s2 = net.send(part(across).at[hi], tmp.at[1], left)
    s3 = net.send(part(after).at[hi], got.at[0, hi], right)
    s4 = net.send(part(before).at[lo], got.at[1, lo], left)
    net.got(s1)
    add_into(tmp.at[0], tmp.at[0], part(after).at[lo], half, step)
    s5 = net.send(tmp.at[0], got.at[0, lo], right)
    net.got(s2)
    add_into(tmp.at[1], tmp.at[1], part(before).at[hi], half, step)
    s6 = net.send(tmp.at[1], got.at[1, hi], left)
    for copy in (s3, s4, s5, s6):
        net.got(copy)


def dot(a, b):
    return lax.dot_general(a, b, (((1,), (0,)), ((), ())), preferred_element_type=f32)


def dot_t(a, b):
    return lax.dot_general(a, b, (((1,), (1,)), ((), ())), preferred_element_type=f32)


def t_dot(a, b):
    return lax.dot_general(a, b, (((0,), (0,)), ((), ())), preferred_element_type=f32)


def gather_kernel(xl, gl, rl, wq, wo, gu, dn, X, R, G, WQ, WO, GU, DN, ss, rs, ls):
    x, y, z, c = place()
    z_hi = z // 2
    shard = z_hi * 4 + y
    slot = x * 2 + c
    net = Net(ss, rs, ls)
    partner = dev(x, y, z + 2, c)
    twin = dev(x, y, z, 1 - c)
    right, left = dev(x + 1, y, z, c), dev(x - 1, y, z, c)
    offsets = [(0, 1), (0, 3), (1, 0), (0, 2), (1, 1), (1, 3), (1, 2)]
    peers = [dev(x, y + dy, (3 - z) if dz else z, c) for dz, dy in offsets]
    net.greet(peers + [partner, twin, right, left])
    rows_of = lambda n: pl.ds(pl.multiple_of(n * 128, 128), 128)
    mine = rows_of(z_hi)
    swaps = [
        net.send(gl.at[1 - z_hi], G.at[slot, mine], partner),
        net.send(xl.at[1 - z_hi], X.at[mine], partner),
        net.send(rl.at[1 - z_hi], R.at[mine], partner),
    ]
    locs = [net.local(gl.at[z_hi], G.at[slot, mine])]
    at = rows_of(shard)
    wq_in = [net.send(wq, WQ.at[c, at], p) for p in peers]
    wo_in = [net.send(wo, WO.at[c, at], p) for p in peers]
    rest = [net.send(gu, GU.at[at], p) for p in peers]
    rest += [net.send(dn, DN.at[:, at], p) for p in peers]
    locs += [
        net.local(xl.at[z_hi], X.at[mine]),
        net.local(rl.at[z_hi], R.at[mine]),
        net.local(wq, WQ.at[c, at]),
        net.local(wo, WO.at[c, at]),
        net.local(gu, GU.at[at]),
        net.local(dn, DN.at[:, at]),
    ]
    net.send(wq, WQ.at[c, at], twin)
    net.send(wo, WO.at[c, at], twin)
    net.got(swaps[0])
    locs[0].wait()
    gpart = lambda n, h: G.at[n * 2 + c, pl.ds(h * 128, 128)]
    ring_gather(net, gpart, right, left, x)
    for n in range(4):
        net.send(G.at[n * 2 + c], G.at[n * 2 + c], twin)
    sources = [
        rows_of((lax.rem(1 - z_hi if dz else z_hi, 2)) * 4 + lax.rem(y + 4 - dy, 4))
        for dz, dy in offsets
    ]
    for copies, whole in ((wq_in, WQ), (wo_in, WO)):
        for copy, src in zip(copies, sources):
            net.got(copy)
            net.send(whole.at[c, src], whole.at[c, src], twin)
    for copy in locs[1:]:
        copy.wait()
    net.finish()


def gather(xl, gl, rl, wq, wo, gu, dn):
    return pl.pallas_call(
        gather_kernel,
        out_shape=(
            shape((ROWS, D), b16),
            shape((ROWS, 128), f32),
            shape((8, ROWS, D), b16),
            shape((2, D, 1024), b16),
            shape((2, D, 512), b16),
            shape((D, 2 * WIDE), b16),
            shape((WIDE + 16, D), b16),
        ),
        in_specs=[ANY] * 7,
        out_specs=(ANY,) * 7,
        scratch_shapes=sems(64, 8),
        compiler_params=params(0),
        name="gather",
    )(xl, gl, rl, wq, wo, gu, dn)


def partner_lanes(v):
    lane = lax.broadcasted_iota(jnp.int32, v.shape, 1)
    return jnp.where(lane % HD < HD // 2, pltpu.roll(v, 96, 1), pltpu.roll(v, 32, 1))


def project_kernel(x, wq, gains, cos, sin, act, q, kv):
    v = x[...].astype(f32)
    gain = gains[6:7, :].astype(f32)
    r = lax.rsqrt(jnp.mean(v * v, axis=-1, keepdims=True) + norm_epsilon)
    a = (v * r * gain).astype(b16)
    act[...] = a
    cosine, sine = cos[...], sin[...]
    for half in range(2):
        for t in range(4):
            out = dot(a, wq[half, :, 256 * t : 256 * (t + 1)])
            for u in range(2):
                tile = out[:, 128 * u : 128 * (u + 1)]
                at = slice(256 * t + 128 * u, 256 * t + 128 * (u + 1))
                if half == 0 or t < 2:
                    tile = tile * cosine + partner_lanes(tile) * sine
                if half == 0:
                    q[:, at] = (tile * 0.125).astype(b16)
                else:
                    kv[:, at] = tile.astype(b16)


def project(x, wq, dn, cos, sin):
    return pl.pallas_call(
        project_kernel,
        grid=(1,),
        out_shape=(shape((ROWS, D), b16),) * 3,
        in_specs=[
            pl.BlockSpec((ROWS, D), lambda i: (0, 0)),
            pl.BlockSpec((2, D, 1024), lambda i: (0, 0, 0)),
            pl.BlockSpec((16, D), lambda i: (WIDE // 16, 0)),
            pl.BlockSpec((ROWS, 128), lambda i: (0, 0)),
            pl.BlockSpec((ROWS, 128), lambda i: (0, 0)),
        ],
        out_specs=(pl.BlockSpec((ROWS, D), lambda i: (0, 0)),) * 3,
        compiler_params=params(),
        name="project",
    )(x, wq, dn, cos, sin)


def keys_kernel(kv, KV, ss, rs, ls):
    x, y, z, c = place()
    net = Net(ss, rs, ls)
    right, left = dev(x, y + 1, z, c), dev(x, y - 1, z, c)
    net.greet([right, left])
    own = net.local(kv, KV.at[y])
    part = lambda n, h: KV.at[n, pl.ds(h * 128, 128)]
    ring_gather(net, part, right, left, y, src=lambda h: kv.at[pl.ds(h * 128, 128)])
    own.wait()
    net.finish()


def gather_keys(kv):
    return pl.pallas_call(
        keys_kernel,
        out_shape=shape((4, ROWS, D), b16),
        in_specs=[ANY],
        out_specs=ANY,
        scratch_shapes=sems(8),
        compiler_params=params(1),
        name="gather_keys",
    )(kv)


def half_mask(rows, half):
    lane = lax.broadcasted_iota(jnp.int32, (rows, 128), 1)
    return (lane < HD) if half == 0 else (lane >= HD)


def spread(tile, half):
    keep = half_mask(ROWS, half)
    heads = []
    for g in range(2):
        v = tile if g == half else pltpu.roll(tile, HD, 1)
        heads.append(jnp.where(keep, v, 0.0).astype(b16))
    low = jnp.concatenate([h[:128] for h in heads], axis=0)
    high = jnp.concatenate([h[128:] for h in heads], axis=0)
    return low, high


def collect(low, high, half):
    heads = []
    for g in range(2):
        v = jnp.concatenate([low[g * 128 : g * 128 + 128], high[g * 128 : g * 128 + 128]], axis=0)
        heads.append(v if g == half else pltpu.roll(v, HD, 1))
    return jnp.where(half_mask(ROWS, 0), heads[0], heads[1])


def attend_kernel(q, k, v, posq, segq, segk, o, p, bias):
    @pl.when(pl.program_id(0) == 0)
    def _():
        place_k = lax.broadcasted_iota(jnp.int32, (128, D), 1)
        for h in range(2):
            at = slice(128 * h, 128 * h + 128)
            fine = (posq[at, :] >= place_k) & (segq[at, :] == segk[...])
            bias[at, :] = jnp.where(fine, 0.0, -1e30)

    keys = [k[:, :128].reshape(512, 128), k[:, 128:].reshape(512, 128)]
    vals = [v[:, :128].reshape(512, 128), v[:, 128:].reshape(512, 128)]
    keys_all = jnp.concatenate(keys, axis=0)
    vals_all = jnp.concatenate(vals, axis=0)
    low_bias = jnp.concatenate([bias[:128, :512]] * 2, axis=0)
    high_bias = jnp.concatenate([bias[128:, :]] * 2, axis=0)
    for half in range(2):
        tile = q[:, 128 * half : 128 * half + 128].astype(f32)
        low, high = spread(tile, half)
        outs = []
        for rows, kk, vv, bb, lo in (
            (low, keys[0], vals[0], low_bias, True),
            (high, keys_all, vals_all, high_bias, False),
        ):
            s = dot_t(rows, kk) + bb
            top = jnp.max(s, axis=-1, keepdims=True)
            e = jnp.exp(s - top)
            probs = (e * (1.0 / jnp.sum(e, axis=-1, keepdims=True))).astype(b16)
            if lo:
                p[half, :, :512] = probs
            else:
                p[half, :, 512:] = probs
            outs.append(dot(probs, vv))
        o[:, 128 * half : 128 * half + 128] = collect(outs[0], outs[1], half).astype(b16)


def attend(q, KV, posq, segq, segk):
    return pl.pallas_call(
        attend_kernel,
        grid=(4,),
        out_shape=(shape((ROWS, D), b16), shape((8, ROWS, 1536), b16)),
        in_specs=[
            pl.BlockSpec((ROWS, 256), lambda i: (0, i)),
            pl.BlockSpec((4, ROWS, 128), lambda i: (0, 0, i)),
            pl.BlockSpec((4, ROWS, 128), lambda i: (0, 0, 4 + i)),
            pl.BlockSpec((ROWS, 1), lambda i: (0, 0)),
            pl.BlockSpec((ROWS, 1), lambda i: (0, 0)),
            pl.BlockSpec((1, D), lambda i: (0, 0)),
        ],
        out_specs=(
            pl.BlockSpec((ROWS, 256), lambda i: (0, i)),
            pl.BlockSpec((2, ROWS, 1536), lambda i: (i, 0, 0)),
        ),
        scratch_shapes=[pltpu.VMEM((ROWS, D), f32)],
        compiler_params=params(),
        name="attend",
    )(q, KV, KV, posq, segq, segk)


def router_rows(tail):
    row = lax.broadcasted_iota(jnp.int32, (16, D), 0)
    kept = jnp.where(row < EXPERTS, tail.astype(f32), 0.0).astype(b16)
    return jnp.concatenate([kept, jnp.zeros((112, D), b16)], axis=0)


def one_hot(routes, slot):
    lane = lax.broadcasted_iota(jnp.int32, (ROWS, 128), 1).astype(f32)
    return (routes[:, slot : slot + 1] == lane).astype(f32)


def after_kernel(x, o, wo, tail, routes, hidden, act):
    heads = o[...]
    for half in range(2):
        for t in range(2):
            cols = slice(512 * half + 256 * t, 512 * half + 256 * (t + 1))
            hidden[:, cols] = x[:, cols].astype(f32) + dot(heads, wo[half, :, 256 * t : 256 * (t + 1)])
    h = hidden[...]
    r = lax.rsqrt(jnp.mean(h * h, axis=-1, keepdims=True) + norm_epsilon)
    a = (h * r * tail[7:8, :].astype(f32)).astype(b16)
    act[:, :D] = a
    logits = dot_t(a, router_rows(tail[...]))
    hots = [one_hot(routes, k) for k in range(TOPK)]
    picked = [jnp.sum(hot * logits, axis=-1, keepdims=True) for hot in hots]
    top = jnp.maximum(picked[0], picked[1])
    powers = [jnp.exp(v - top) for v in picked]
    total = powers[0] + powers[1]
    mixing = hots[0] * (powers[0] / total) + hots[1] * (powers[1] / total)
    big = mixing.astype(b16).astype(f32)
    act[:, D:] = (big + pltpu.roll(mixing - big, 16, 1)).astype(b16)


def after(x, o, wo, dn, routes):
    return pl.pallas_call(
        after_kernel,
        grid=(1,),
        out_shape=(shape((ROWS, D), f32), shape((ROWS, D + 128), b16)),
        in_specs=[
            pl.BlockSpec((ROWS, D), lambda i: (0, 0)),
            pl.BlockSpec((ROWS, D), lambda i: (0, 0)),
            pl.BlockSpec((2, D, 512), lambda i: (0, 0, 0)),
            pl.BlockSpec((16, D), lambda i: (WIDE // 16, 0)),
            pl.BlockSpec((ROWS, 128), lambda i: (0, 0)),
        ],
        out_specs=(
            pl.BlockSpec((ROWS, D), lambda i: (0, 0)),
            pl.BlockSpec((ROWS, D + 128), lambda i: (0, 0)),
        ),
        compiler_params=params(),
        name="after_attention",
    )(x, o, wo, dn, routes)


def tokens_kernel(act, ACT, ss, rs, ls):
    x, y, z, c = place()
    net = Net(ss, rs, ls)
    right, left, twin = dev(x + 1, y, z, c), dev(x - 1, y, z, c), dev(x, y, z, 1 - c)
    net.greet([right, left, twin])
    own = net.local(act, ACT.at[x * 2 + c])
    net.send(act, ACT.at[x * 2 + c], twin)
    part = lambda n, h: ACT.at[n * 2 + c, pl.ds(h * 128, 128)]
    ring_gather(net, part, right, left, x, src=lambda h: act.at[pl.ds(h * 128, 128)])
    for d in range(1, 4):
        block = ACT.at[lax.rem(x + d, 4) * 2 + c]
        net.send(block, block, twin)
    own.wait()
    net.finish()


def gather_tokens(act):
    return pl.pallas_call(
        tokens_kernel,
        out_shape=shape((8, ROWS, D + 128), b16),
        in_specs=[ANY],
        out_specs=ANY,
        scratch_shapes=sems(16),
        compiler_params=params(2),
        name="gather_tokens",
    )(act)


def experts_kernel(act, g, gu, dn, part, grads, gu_acc, dn_acc):
    step = pl.program_id(0)
    row = lax.broadcasted_iota(jnp.int32, (128, WIDE), 0)
    lane = lax.broadcasted_iota(jnp.int32, (128, WIDE), 1)
    pick = ((row % 16 == lane // SLICE) & (row < 32)).astype(b16)
    a = act[0, :, :D]
    mix = dot(act[0, :, D:], pick)
    gt = g[0]
    down = dn[:WIDE, :]
    h = dot(a, gu[...])
    gate, up = h[:, :WIDE], h[:, WIDE:]
    gw = dot_t(gt, down)
    s = 1.0 / (1.0 + jnp.exp(-gate))
    silu = gate * s
    inner = silu * up
    scaled = (inner * mix).astype(b16)
    part[0, :, :D] = dot(scaled, down).astype(b16)
    part[0, :, 2 * D :] = dot_t((inner * gw).astype(b16), pick).astype(b16)
    gi = gw * mix
    ggu = jnp.concatenate(
        [(gi * up * s * (1.0 + gate * (1.0 - s))).astype(b16), (gi * silu).astype(b16)], axis=1
    )
    part[0, :, D : 2 * D] = dot_t(ggu, gu[...]).astype(b16)

    @pl.when(step == 0)
    def _():
        gu_acc[...] = jnp.zeros_like(gu_acc)
        dn_acc[...] = jnp.zeros_like(dn_acc)

    gu_acc[...] += t_dot(a, ggu)
    dn_acc[...] += t_dot(scaled, gt)

    @pl.when(step == 7)
    def _():
        for n in range(8):
            at = slice(128 * n, 128 * n + 128)
            for b in range(6):
                grads[n, b] = gu_acc[at, 128 * b : 128 * b + 128].astype(b16)
            for b in range(3):
                grads[n, 6 + b] = dn_acc[128 * b : 128 * b + 128, at].astype(b16)


def experts(ACT, G, GU, DN):
    return pl.pallas_call(
        experts_kernel,
        grid=(8,),
        out_shape=(shape((8, ROWS, 2 * D + 128), b16), shape((8, 9, 128, 128), b16)),
        in_specs=[
            pl.BlockSpec((1, ROWS, D + 128), lambda i: (i, 0, 0)),
            pl.BlockSpec((1, ROWS, D), lambda i: (i, 0, 0)),
            pl.BlockSpec((D, 2 * WIDE), lambda i: (0, 0)),
            pl.BlockSpec((WIDE + 16, D), lambda i: (0, 0)),
        ],
        out_specs=(
            pl.BlockSpec((1, ROWS, 2 * D + 128), lambda i: (i, 0, 0)),
            pl.BlockSpec((8, 9, 128, 128), lambda i: (0, 0, 0, 0)),
        ),
        scratch_shapes=[pltpu.VMEM((D, 2 * WIDE), f32), pltpu.VMEM((WIDE, D), f32)],
        compiler_params=params(),
        name="experts",
    )(ACT, G, GU, DN)


def home_kernel(part, total, twin_got, tmp, got, ss, rs, ls):
    x, y, z, c = place()
    net = Net(ss, rs, ls)
    right, left, twin = dev(x + 1, y, z, c), dev(x - 1, y, z, c), dev(x, y, z, 1 - c)
    net.greet([right, left, twin])
    order = [lax.rem(x + d, 4) for d in (2, 1, 3, 0)]
    sent = [net.send(part.at[n * 2 + 1 - c], twin_got.at[n], twin) for n in order]
    for n, copy in zip(order, sent):
        net.got(copy)
        add_into(twin_got.at[n], twin_got.at[n], part.at[n * 2 + c], ROWS, 16)
    ring_scatter(net, lambda n: twin_got.at[n], tmp, got, right, left, x, ROWS, 16)

    def body(i, carry):
        at = pl.ds(pl.multiple_of(i * 16, 16), 16)
        total[at] = twin_got[x, at].astype(f32) + got[0, at].astype(f32) + got[1, at].astype(f32)
        return carry

    lax.fori_loop(0, ROWS // 16, body, 0)
    net.finish()


def send_home(part):
    wide = 2 * D + 128
    return pl.pallas_call(
        home_kernel,
        out_shape=shape((ROWS, wide), f32),
        in_specs=[VMEM],
        out_specs=VMEM,
        scratch_shapes=[
            pltpu.VMEM((4, ROWS, wide), b16),
            pltpu.VMEM((2, ROWS // 2, wide), b16),
            pltpu.VMEM((2, ROWS, wide), b16),
        ]
        + sems(16),
        compiler_params=params(3),
        name="send_home",
    )(part)


def middle_kernel(total, hidden, act, g, tail, routes, heads, wo, out, gh_ref, ghi, og, small):
    h = hidden[...]
    out[...] = (h + total[:, :D]).astype(b16)
    a = act[:, :D]
    mix = act[:, D:].astype(f32)
    lane = lax.broadcasted_iota(jnp.int32, (ROWS, 128), 1)
    mixing = jnp.where(lane < 16, mix + pltpu.roll(mix, 112, 1), 0.0)
    dg = total[:, 2 * D :]
    hots = [one_hot(routes, k) for k in range(TOPK)]
    probs = [jnp.sum(hot * mixing, axis=-1, keepdims=True) for hot in hots]
    dgs = [jnp.sum(hot * dg, axis=-1, keepdims=True) for hot in hots]
    mean = probs[0] * dgs[0] + probs[1] * dgs[1]
    grad_logits = sum(hot * (p * (d - mean)) for hot, p, d in zip(hots, probs, dgs)).astype(b16)
    ga = total[:, D : 2 * D] + dot(grad_logits, router_rows(tail[...]))
    small[0:6, :] = t_dot(grad_logits, a)[0:6, :]
    r = lax.rsqrt(jnp.mean(h * h, axis=-1, keepdims=True) + norm_epsilon)
    u = ga * tail[7:8, :].astype(f32)
    small[6:7, :] = jnp.sum(ga * h * r, axis=0, keepdims=True)
    small[7:8, :] = jnp.zeros((1, D), f32)
    gh = g[0].astype(f32) + r * (u - h * (r * r * jnp.mean(u * h, axis=-1, keepdims=True)))
    gh_ref[...] = gh
    low = gh.astype(b16)
    ghi[...] = (dot_t(low[:, :512], wo[0]) + dot_t(low[:, 512:], wo[1])).astype(b16)
    o = heads[...]
    for k in range(8):
        piece = t_dot(o, low[:, 128 * k : 128 * k + 128]).astype(b16)
        for n in range(8):
            og[k, n, 0] = piece[128 * n : 128 * n + 128]


def middle(slot, total, hidden, act, G, dn, routes, heads, wo):
    whole = lambda *dims: pl.BlockSpec(dims, lambda i, s: (0,) * len(dims))
    return pl.pallas_call(
        middle_kernel_with_slot,
        grid_spec=pltpu.PrefetchScalarGridSpec(
            num_scalar_prefetch=1,
            grid=(1,),
            in_specs=[
                whole(ROWS, 2 * D + 128),
                whole(ROWS, D),
                whole(ROWS, D + 128),
                pl.BlockSpec((1, ROWS, D), lambda i, s: (s[0], 0, 0)),
                pl.BlockSpec((16, D), lambda i, s: (WIDE // 16, 0)),
                whole(ROWS, 128),
                whole(ROWS, D),
                whole(2, D, 512),
            ],
            out_specs=(
                whole(ROWS, D),
                whole(ROWS, D),
                whole(ROWS, D),
                whole(8, 8, 1, 128, 128),
                whole(8, D),
            ),
        ),
        out_shape=(
            shape((ROWS, D), b16),
            shape((ROWS, D), f32),
            shape((ROWS, D), b16),
            shape((8, 8, 1, 128, 128), b16),
            shape((8, D), f32),
        ),
        compiler_params=params(),
        name="middle",
    )(slot, total, hidden, act, G, dn, routes, heads, wo)


def middle_kernel_with_slot(slot, *refs):
    middle_kernel(*refs)


def attend_back_kernel(q, k, v, p, do, dq, dk, dv):
    keys = [k[:, :128].reshape(512, 128), k[:, 128:].reshape(512, 128)]
    vals = [v[:, :128].reshape(512, 128), v[:, 128:].reshape(512, 128)]
    keys_all = jnp.concatenate(keys, axis=0)
    vals_all = jnp.concatenate(vals, axis=0)
    dk_sum = dv_sum = None
    for half in range(2):
        at = slice(128 * half, 128 * half + 128)
        q_low, q_high = spread(q[:, at].astype(f32), half)
        do_low, do_high = spread(do[:, at].astype(f32), half)
        outs, dks, dvs = [], [], []
        for qq, dd, kk, vv, cols in (
            (q_low, do_low, keys[0], vals[0], slice(0, 512)),
            (q_high, do_high, keys_all, vals_all, slice(512, 1536)),
        ):
            probs = p[half, :, cols]
            dp = dot_t(dd, vv)
            pf = probs.astype(f32)
            prod = pf * dp
            ds = (prod - pf * jnp.sum(prod, axis=-1, keepdims=True)).astype(b16)
            outs.append(dot(ds, kk) * 0.125)
            dks.append(t_dot(ds, qq))
            dvs.append(t_dot(probs, dd))
        dq[:, at] = collect(outs[0], outs[1], half)
        if half == 0:
            dk_sum, dv_sum = dks, dvs
        else:
            dk_sum = [a + b for a, b in zip(dk_sum, dks)]
            dv_sum = [a + b for a, b in zip(dv_sum, dvs)]
    for ref, (low, whole) in ((dk, dk_sum), (dv, dv_sum)):
        ref[:, :128] = (low + whole[:512]).reshape(4, 128, 128).astype(b16)
        ref[:, 128:] = whole[512:].reshape(4, 128, 128).astype(b16)


def attend_back(q, KV, p, do):
    return pl.pallas_call(
        attend_back_kernel,
        grid=(4,),
        out_shape=(shape((ROWS, D), f32), shape((4, ROWS, 512), b16), shape((4, ROWS, 512), b16)),
        in_specs=[
            pl.BlockSpec((ROWS, 256), lambda i: (0, i)),
            pl.BlockSpec((4, ROWS, 128), lambda i: (0, 0, i)),
            pl.BlockSpec((4, ROWS, 128), lambda i: (0, 0, 4 + i)),
            pl.BlockSpec((2, ROWS, 1536), lambda i: (i, 0, 0)),
            pl.BlockSpec((ROWS, 256), lambda i: (0, i)),
        ],
        out_specs=(
            pl.BlockSpec((ROWS, 256), lambda i: (0, i)),
            pl.BlockSpec((4, ROWS, 128), lambda i: (0, 0, i)),
            pl.BlockSpec((4, ROWS, 128), lambda i: (0, 0, i)),
        ),
        compiler_params=params(),
        name="attend_back",
    )(q, KV, KV, p, do)


def keys_home_kernel(dk, dv, out, ktmp, kgot, vtmp, vgot, ss, rs, ls):
    x, y, z, c = place()
    net = Net(ss, rs, ls)
    right, left = dev(x, y + 1, z, c), dev(x, y - 1, z, c)
    net.greet([right, left])
    ring_scatter(net, lambda n: dk.at[n], ktmp, kgot, right, left, y, ROWS, 32)
    ring_scatter(net, lambda n: dv.at[n], vtmp, vgot, right, left, y, ROWS, 32)
    out[:, :512] = dk[y].astype(f32) + kgot[0].astype(f32) + kgot[1].astype(f32)
    out[:, 512:] = dv[y].astype(f32) + vgot[0].astype(f32) + vgot[1].astype(f32)
    net.finish()


def keys_home(dk, dv):
    return pl.pallas_call(
        keys_home_kernel,
        out_shape=shape((ROWS, D), f32),
        in_specs=[VMEM] * 2,
        out_specs=VMEM,
        scratch_shapes=[
            pltpu.VMEM((2, ROWS // 2, 512), b16),
            pltpu.VMEM((2, ROWS, 512), b16),
        ]
        * 2
        + sems(16),
        compiler_params=params(4),
        name="keys_home",
    )(dk, dv)


def project_back_kernel(dq, dkv, x, act, gh_ref, wq, tail, cos, sin, gin, qg, small, gp):
    cosine, sine = cos[...], sin[...]
    for t in range(16):
        src = dq if t < 8 else dkv
        at = slice(128 * (t % 8), 128 * (t % 8) + 128)
        tile = src[:, at]
        if t < 12:
            tile = tile * cosine - partner_lanes(tile) * sine
        gp[:, 128 * t : 128 * t + 128] = tile.astype(b16)
    ga = dot_t(gp[:, :D], wq[0]) + dot_t(gp[:, D:], wq[1])
    v = x[...].astype(f32)
    r = lax.rsqrt(jnp.mean(v * v, axis=-1, keepdims=True) + norm_epsilon)
    u = ga * tail[6:7, :].astype(f32)
    small[...] = jnp.sum(ga * v * r, axis=0, keepdims=True)
    gin[...] = gh_ref[...] + r * (u - v * (r * r * jnp.mean(u * v, axis=-1, keepdims=True)))
    a = act[...]
    for k in range(8):
        piece = t_dot(a, gp[:, 256 * k : 256 * k + 256]).astype(b16)
        for n in range(8):
            for b in range(2):
                qg[k, n, b] = piece[128 * n : 128 * n + 128, 128 * b : 128 * b + 128]


def project_back(dq, dkv, x, act, gh, wq, dn, cos, sin):
    whole = lambda *dims: pl.BlockSpec(dims, lambda i: (0,) * len(dims))
    return pl.pallas_call(
        project_back_kernel,
        grid=(1,),
        out_shape=(
            shape((ROWS, D), f32),
            shape((8, 8, 2, 128, 128), b16),
            shape((1, D), f32),
        ),
        in_specs=[
            whole(ROWS, D),
            whole(ROWS, D),
            whole(ROWS, D),
            whole(ROWS, D),
            whole(ROWS, D),
            whole(2, D, 1024),
            pl.BlockSpec((16, D), lambda i: (WIDE // 16, 0)),
            whole(ROWS, 128),
            whole(ROWS, 128),
        ],
        out_specs=(whole(ROWS, D), whole(8, 8, 2, 128, 128), whole(1, D)),
        scratch_shapes=[pltpu.VMEM((ROWS, 2 * D), b16)],
        compiler_params=params(),
        name="project_back",
    )(dq, dkv, x, act, gh, wq, dn, cos, sin)


def reduce_kernel(
    grads, og, qg, small, out, gin, ALL, SM, OUT, GIN,
    mine, o_twin, q_twin, o_tmp, o_got, q_tmp, q_got, y_tmp, y_got, z_got, half, s_twin, s_x, s_y, s_z, gin_low, gin_got,
    ss, rs, ls,
):
    x, y, z, c = place()
    z_hi, z_lo = z // 2, lax.rem(z, 2)
    net = Net(ss, rs, ls)
    twin = dev(x, y, z, 1 - c)
    xr, xl = dev(x + 1, y, z, c), dev(x - 1, y, z, c)
    x2 = dev(x + 2, y, z, c)
    yr, yl, y2 = dev(x, y + 1, z, c), dev(x, y - 1, z, c), dev(x, y + 2, z, c)
    zr, zl, z2 = dev(x, y, z + 1, c), dev(x, y, z - 1, c), dev(x, y, z + 2, c)
    net.greet([twin, xr, xl, x2, yr, yl, y2, zr, zl, z2])
    rows_of = lambda n: pl.ds(pl.multiple_of(n * 128, 128), 128)
    gin_low[...] = gin[rows_of(1 - z_hi)].astype(b16)
    net.send(out.at[rows_of(1 - z_hi)], OUT.at[z_hi], z2)
    swap = net.send(gin_low, gin_got, z2)
    OUT[z_hi] = out[rows_of(z_hi)]
    GIN[z_hi] = gin[rows_of(z_hi)]
    og_sent = [net.send(og.at[n * 2 + 1 - c], o_twin.at[n], twin) for n in range(4)]
    qg_sent = [net.send(qg.at[n * 2 + 1 - c], q_twin.at[n], twin) for n in range(4)]
    sm = net.send(small, s_twin, twin)
    for n in range(4):
        net.got(og_sent[n])
        add_into(o_twin.at[n], o_twin.at[n], og.at[n * 2 + c], 8, 1)
    for n in range(4):
        net.got(qg_sent[n])
        add_into(q_twin.at[n], q_twin.at[n], qg.at[n * 2 + c], 8, 1)
    net.got(sm)
    s_twin[...] += small[...]
    sx = [net.send(s_twin, s_x.at[i], p) for i, p in enumerate((xr, xl, x2))]
    ring_scatter(net, lambda n: o_twin.at[n], o_tmp, o_got, xr, xl, x, 8, 1)
    ring_scatter(net, lambda n: q_twin.at[n], q_tmp, q_got, xr, xl, x, 8, 1)

    def fill(n, carry):
        mine[n, 0:9] = grads[n]
        mine[n, 9:10] = (o_twin[x, n].astype(f32) + o_got[0, n].astype(f32) + o_got[1, n].astype(f32)).astype(b16)
        mine[n, 10:12] = (q_twin[x, n].astype(f32) + q_got[0, n].astype(f32) + q_got[1, n].astype(f32)).astype(b16)
        return carry

    lax.fori_loop(0, 8, fill, 0)
    for copy in sx:
        net.got(copy)
    s_y[0] = s_twin[...] + s_x[0] + s_x[1] + s_x[2]
    sy = [net.send(s_y.at[0], s_y.at[1 + i], p) for i, p in enumerate((yr, yl, y2))]
    for h in range(2):
        ring_scatter(net, lambda n: mine.at[h * 4 + n], y_tmp.at[h], y_got.at[h], yr, yl, y, 12, 1)

        def settle(b, carry):
            mine[h * 4 + y, b] = (
                mine[h * 4 + y, b].astype(f32) + y_got[h, 0, b].astype(f32) + y_got[h, 1, b].astype(f32)
            ).astype(b16)
            return carry

        lax.fori_loop(0, 12, settle, 0)
    for copy in sy:
        net.got(copy)
    s_z[0] = s_y[0] + s_y[1] + s_y[2] + s_y[3]
    sz = [net.send(s_z.at[0], s_z.at[1 + i], p) for i, p in enumerate((zr, zl, z2))]

    def piece(zz):
        return mine.at[(zz // 2) * 4 + y, pl.ds(lax.rem(zz, 2) * 6, 6)]

    zs = [
        net.send(piece(lax.rem(z + 1, 4)), z_got.at[0], zr),
        net.send(piece(lax.rem(z + 3, 4)), z_got.at[1], zl),
        net.send(piece(lax.rem(z + 2, 4)), z_got.at[2], z2),
    ]
    for copy in zs:
        net.got(copy)
    base = z_hi * 4 + y
    slot = x * 2 + c

    def settle_z(b, carry):
        at = z_lo * 6 + b
        v = mine[base, at].astype(f32) + z_got[0, b].astype(f32) + z_got[1, b].astype(f32) + z_got[2, b].astype(f32)
        ALL[slot, at] = v.astype(b16)
        return carry

    lax.fori_loop(0, 6, settle_z, 0)
    for copy in sz:
        net.got(copy)
    SM[...] = s_z[0] + s_z[1] + s_z[2] + s_z[3]
    done = ALL.at[slot, pl.ds(z_lo * 6, 6)]
    hop = dev(x, y, z + 1 - 2 * z_lo, c)
    net.got(net.send(done, done, hop))
    block = ALL.at[slot]
    net.send(block, block, twin)
    part = lambda n, h: ALL.at[n * 2 + c, pl.ds(h * 6, 6)]
    ring_gather(net, part, xr, xl, x)
    for d in range(1, 4):
        block = ALL.at[lax.rem(x + d, 4) * 2 + c]
        net.send(block, block, twin)
    net.got(swap)
    GIN[1 - z_hi] = gin_got[...].astype(f32)
    net.finish()


def reduce_all(grads, og, qg, small, out, gin):
    return pl.pallas_call(
        reduce_kernel,
        out_shape=(
            shape((8, 12, 128, 128), b16),
            shape((8, D), f32),
            shape((2, 128, D), b16),
            shape((2, 128, D), f32),
        ),
        in_specs=[VMEM] * 6,
        out_specs=(VMEM,) * 4,
        scratch_shapes=[
            pltpu.VMEM((8, 12, 128, 128), b16),
            pltpu.VMEM((4, 8, 1, 128, 128), b16),
            pltpu.VMEM((4, 8, 2, 128, 128), b16),
            pltpu.VMEM((2, 4, 1, 128, 128), b16),
            pltpu.VMEM((2, 8, 1, 128, 128), b16),
            pltpu.VMEM((2, 4, 2, 128, 128), b16),
            pltpu.VMEM((2, 8, 2, 128, 128), b16),
            pltpu.VMEM((2, 2, 6, 128, 128), b16),
            pltpu.VMEM((2, 2, 12, 128, 128), b16),
            pltpu.VMEM((3, 6, 128, 128), b16),
            pltpu.VMEM((6, 128, 128), b16),
            pltpu.VMEM((8, D), f32),
            pltpu.VMEM((3, 8, D), f32),
            pltpu.VMEM((4, 8, D), f32),
            pltpu.VMEM((4, 8, D), f32),
            pltpu.VMEM((128, D), b16),
            pltpu.VMEM((128, D), b16),
        ]
        + sems(64),
        compiler_params=params(5),
        name="reduce_all",
    )(grads, og, qg, small, out, gin)


def rotary(positions):
    freqs = 10000.0 ** (-jnp.arange(HD // 2).astype(f32) * 2.0 / HD)
    angles = positions.astype(f32)[:, None] * freqs[None, :]
    cos, sin = jnp.cos(angles), jnp.sin(angles)
    return jnp.concatenate([cos] * 4, axis=1), jnp.concatenate([-sin, sin] * 2, axis=1)


def learning_rates():
    return (D ** (-0.5), 8.0 * D ** (-0.5), D ** (-0.5), 2.0 * FF ** (-0.5), 0.5 * D ** (-0.5), 0.5)


def adamw(weight, gradient, moment, square, step_rate, decay_rate):
    moment_new = beta_one * moment + (1.0 - beta_one) * gradient
    square_new = beta_two * square + (1.0 - beta_two) * gradient * gradient
    corrected = moment_new / (1.0 - beta_one**STEP)
    spread_by = jnp.sqrt(square_new / (1.0 - beta_two**STEP)) + adam_epsilon
    updated = weight - step_rate * (corrected / spread_by + decay_rate * weight)
    return [moment_new, square_new, updated]


def on_device(
    tokens, segments, routes, cotangent, w_qkv, w_out, w_gateup, w_down, w_router, w_gains,
    qkv_first, qkv_second, out_first, out_second, gateup_first, gateup_second, down_first, down_second,
    router_first, router_second, gains_first, gains_second,
):
    x, y, z, c = place()
    z_hi = z // 2
    slot = x * 2 + c
    shard = z_hi * 4 + y
    cut = lax.dynamic_slice_in_dim
    wq = cut(w_qkv, c * 1024, 1024, 1).astype(b16)
    wo = cut(w_out, c * 512, 512, 1).astype(b16)
    gate = cut(w_gateup, slot * SLICE, SLICE, 2)
    up = cut(w_gateup, FF + slot * SLICE, SLICE, 2)
    gu = jnp.concatenate(
        [v.astype(b16).transpose(1, 0, 2).reshape(128, WIDE) for v in (gate, up)], axis=1
    )
    dn = jnp.concatenate(
        [
            cut(w_down, slot * SLICE, SLICE, 1).reshape(WIDE, 128),
            w_router.T,
            w_gains,
            jnp.zeros((8, 128), f32),
        ],
        axis=0,
    ).astype(b16)
    route_lanes = jnp.pad(routes.astype(f32), ((0, 0), (0, 0), (0, 126)))
    X, R, G, WQ, WO, GU, DN = gather(tokens, cotangent, route_lanes, wq, wo, gu, dn)

    posq = jnp.concatenate([y * 128 + jnp.arange(128), 512 + y * 128 + jnp.arange(128)])
    cos, sin = rotary(posq)
    seg = lax.dynamic_index_in_dim(segments, z_hi, 0, keepdims=False)
    segq = jnp.concatenate([cut(seg, y * 128, 128, 0), cut(seg, 512 + y * 128, 128, 0)])

    act_one, q, kv = project(X, WQ, DN, cos, sin)
    KV = gather_keys(kv)
    heads, probs = attend(q, KV, posq[:, None], segq[:, None], seg[None, :])
    hidden, act = after(X, heads, WO, DN, R)
    ACT = gather_tokens(act)
    part, grads = experts(ACT, G, GU, DN)
    total = send_home(part)
    out, gh, ghi, og, small_two = middle(slot[None], total, hidden, act, G, DN, R, heads, WO)
    dq, dk, dv = attend_back(q, KV, probs, ghi)
    dkv = keys_home(dk, dv)
    gin, qg, small_one = project_back(dq, dkv, X, act_one, gh, WQ, DN, cos, sin)
    small = jnp.concatenate([small_two[:7], small_one], axis=0)
    ALL, SM, layer_out, input_grad = reduce_all(grads, og, qg, small, out, gin)

    ALL = ALL.astype(f32)
    gate_up = [
        ALL[:, b : b + 3].reshape(8, 3, 128, 2, SLICE).transpose(1, 3, 2, 0, 4).reshape(EXPERTS, 128, FF)
        for b in (0, 3)
    ]
    mine = cut(SM, shard * 128, 128, 1)
    summed = (
        ALL[:, 10:12].transpose(2, 0, 1, 3).reshape(128, 2 * D),
        ALL[:, 9].transpose(1, 0, 2).reshape(128, D),
        jnp.concatenate(gate_up, axis=2),
        ALL[:, 6:9].reshape(8, EXPERTS, SLICE, 128).transpose(1, 0, 2, 3).reshape(EXPERTS, FF, 128),
        mine[:6].T,
        jnp.stack([mine[7], mine[6]]),
    )
    masters = (w_qkv, w_out, w_gateup, w_down, w_router, w_gains)
    firsts = (qkv_first, out_first, gateup_first, down_first, router_first, gains_first)
    seconds = (qkv_second, out_second, gateup_second, down_second, router_second, gains_second)
    decays = (0.1, 0.1, 0.1, 0.1, 0.1, 0.0)
    results = []
    for n in range(6):
        results += adamw(masters[n], summed[n], firsts[n], seconds[n], learning_rates()[n], decays[n])
    return (layer_out, input_grad, *results)


def solution(mesh):
    weight = [P("grp", None), P("grp", None), P(None, "grp", None), P(None, None, "grp"), P("grp", None), P(None, "grp")]
    tokens = P("rep", "grp", None)
    moments = [spec for spec in weight for _ in range(2)]
    results = [spec for spec in weight for _ in range(3)]
    return jax.shard_map(
        on_device,
        mesh=mesh,
        in_specs=(tokens, P("rep", None), tokens, tokens, *weight, *moments),
        out_specs=(tokens, tokens, *results),
        check_vma=False,
    )
```

time: 1470 us -> 490 us (0.33)
  waiting for transfers between devices: 1050 us -> 0 us
  Pallas kernels: 0 us -> 392 us
  matrix products: 144 us -> 0 us
  blocking collectives: 76.4 us -> 0 us
  local copies, waits for them, and re-layouts: 131 us -> 70.8 us
  other arithmetic: 46.4 us -> 25 us
    pallas_call x0 -> x13, Pallas kernels: none -> 392 us  [the longest x1 111 us: reduce_all(): pl.pallas_call(reduce_kernel, out_shape=(shape((8, 12, 128, 128), b16), s...]
    all_gather x6 -> x0, waiting for transfers between devices: 381 us -> none  [the longest x1 147 us: on_device(): lax.all_gather(w_gateup.astype(b16), 'grp', axis=1, tiled=True)]
    unnamed x20 -> x0, waiting for transfers between devices: 376 us -> none
    reduce_scatter x3 -> x0, waiting for transfers between devices: 191 us -> none  [the longest x1 87.9 us: on_device(): lax.psum_scatter(qkv_grad.astype(jnp.bfloat16), 'grp', scatter_dimension=...]
    dot_general x21 -> x0, matrix products: 144 us -> none  [the longest x1 24.1 us: on_device(): jnp.einsum('bhgqk,bqhgd->bkhd', grad_raw, queries, preferred_element_type...]
    psum x1 -> x0, waiting for transfers between devices: 99.9 us -> none  [on_device(): lax.psum(summed[0].astype(jnp.bfloat16), 'rep').astype(jnp.float32)]
    unnamed x128 -> x60, local copies, waits for them, and re-layouts: 108 us -> 43.7 us
    all_gather x2 -> x0, blocking collectives: 47.3 us -> none  [the longest x1 25.9 us: on_device(): lax.all_gather(w_router.astype(b16), 'grp', axis=0, tiled=True)]
  transfers between devices with their start and end apart: 15 -> 0, of which waited for: 14 -> 0; matrix products, arithmetic and copies ran while one was open for 15% -> 0% of each run, Pallas kernels for 0% -> 0%
where the time goes in v1:
time: 490 us; the launch traced here: 489 us
  Pallas kernels  392 us (80%)
  local copies, waits for them, and re-layouts  70.8 us (14%)
  other arithmetic  25 us (5%)
    pallas_call x1, Pallas kernels, reduce_all(): pl.pallas_call(reduce_kernel, out_shape=(shape((8, 12, 128, 128), b16), s...  111 us
    pallas_call x1, Pallas kernels, gather(): pl.pallas_call(gather_kernel, out_shape=(shape((ROWS, D), b16), shape((RO...  82.1 us
    pallas_call x1, Pallas kernels, send_home(): pl.pallas_call(home_kernel, out_shape=shape((ROWS, wide), f32), in_specs=...  53.1 us
    unnamed x60, local copies, waits for them, and re-layouts  43.7 us
    pallas_call x1, Pallas kernels, gather_tokens(): pl.pallas_call(tokens_kernel, out_shape=shape((8, ROWS, D + 128), b16), i...  28.5 us
    pallas_call x1, Pallas kernels, experts(): pl.pallas_call(experts_kernel, grid=(8,), out_shape=(shape((8, ROWS, 2 *...  25.1 us
    pallas_call x1, Pallas kernels, keys_home(): pl.pallas_call(keys_home_kernel, out_shape=shape((ROWS, D), f32), in_spec...  22.2 us
    pallas_call x1, Pallas kernels, gather_keys(): pl.pallas_call(keys_kernel, out_shape=shape((4, ROWS, D), b16), in_specs=...  20.4 us

profile of v1, /device:TPU:1, one launch (start us, length us, event | category | flops | bytes accessed | tf_op | source)
XLA Modules:
  0.0 488.7 jit_solution(10916220014010929158)
XLA Ops:
  13.9 82.1 %gather.1 = (bf16[256,1024]{1,0:T(8,128)(2,1)}, f32[256,128]{1,0:T(8,128)}, bf16[8,256,1024]{2,1,0:T(8,128)(2,1)}, bf16[2,1024,1024]{2,1,0:T(8,128)(2,1)}, bf16[...) custom-call(bf16[2,128,1024]{2,1,0:T(8,128)(2,1)} %xl.1, bf16[2,128,1024]{2,1,0:T(8,128)(2,1)} %gl.1, ...), custom_call_target="tpu_custom_call" | custom-call | tf_op jit(solution)/shard_map/gather/pallas_call | solution.py:221
  96.8 4.6 project.1
  101.4 20.4 %gather_keys.1.k.v = bf16[4,256,1024]{2,1,0:T(8,128)(2,1)} custom-call(bf16[256,1024]{1,0:T(8,128)(2,1)} %get-tuple-element.55.kv), custom_call_target="tpu_custom_call" | custom-call | tf_op jit(solution)/shard_map/gather_keys/pallas_call | solution.py:297
  124.0 11.7 %attend.1 = (bf16[256,1024]{1,0:T(8,128)(2,1)}, bf16[8,256,1536]{2,1,0:T(8,128)(2,1)}) custom-call(bf16[256,1024]{1,0:T(8,128)(2,1)} %get-tuple-element.54.q, bf16[4,256,1024]{2,1,0:T(8,128)(2,1)} %gather_keys.1.k.v, bf16[4,256,1024]{2,1,0:T(8,128)(2,1)} %gather_keys.1.k.v, s32[256,1]{1,0:T(8,128)} %copy.89.posq, s32[256,1]{1,0:T(8,128)} %copy.90.segq, ...), custom_call_target="tpu_custom_call" | custom-call | tf_op jit(solution)/shard_map/attend/pallas_call | solution.py:368
  135.6 4.2 after_attention.1
  139.8 28.5 %gather_tokens.1.act = bf16[8,256,1152]{2,1,0:T(8,128)(2,1)} custom-call(bf16[256,1152]{1,0:T(8,128)(2,1)} %get-tuple-element.59.act.refs_2_), custom_call_target="tpu_custom_call" | custom-call | tf_op jit(solution)/shard_map/gather_tokens/pallas_call | solution.py:460
  168.3 25.1 %experts.1 = (bf16[8,256,2176]{2,1,0:T(8,128)(2,1)}, bf16[8,9,128,128]{3,2,1,0:T(8,128)(2,1)}) custom-call(bf16[8,256,1152]{2,1,0:T(8,128)(2,1)} %gather_tokens.1.act, bf16[8,256,1024]{2,1,0:T(8,128)(2,1)} %get-tuple-element.60.g.refs_3_, bf16[1024,768]{1,0:T(8,128)(2,1)} %get-tuple-element.61.gu, bf16[400,1024]{1,0:T(8,128)(2,1)} %get-tuple-element.53.gains.tail.dn.refs_4_), custom_call_target="tpu_custom_call" | custom-call | tf_op jit(solution)/shard_map/experts/pallas_call | solution.py:514
  193.4 53.1 %send_home.1.refs_0_ = f32[256,2176]{1,0:T(8,128)} custom-call(bf16[8,256,2176]{2,1,0:T(8,128)(2,1)} %get-tuple-element.63.part), custom_call_target="tpu_custom_call" | custom-call | tf_op jit(solution)/shard_map/send_home/pallas_call | solution.py:557
  246.5 7.4 %middle.1 = (bf16[256,1024]{1,0:T(8,128)(2,1)}, f32[256,1024]{1,0:T(8,128)}, bf16[256,1024]{1,0:T(8,128)(2,1)}, bf16[8,8,1,128,128]{4,3,2,1,0:T(8,128)(2,1)}, f32[8,1024]{1,0:T(8,128)}) custom-call(s32[1]{0:T(128)} %bitcast.10.slot, f32[256,2176]{1,0:T(8,128)} %send_home.1.refs_0_, f32[256,1024]{1,0:T(8,128)} %get-tuple-element.64.refs_1_, ...), custom_call_target="tpu_custom_call" | custom-call | tf_op jit(solution)/shard_map/middle/pallas_call | solution.py:605
  253.9 13.2 %attend_back.1 = (f32[256,1024]{1,0:T(8,128)}, bf16[4,256,512]{2,1,0:T(8,128)(2,1)}, bf16[4,256,512]{2,1,0:T(8,128)(2,1)}) custom-call(bf16[256,1024]{1,0:T(8,128)(2,1)} %get-tuple-element.54.q, bf16[4,256,1024]{2,1,0:T(8,128)(2,1)} %gather_keys.1.k.v, bf16[4,256,1024]{2,1,0:T(8,128)(2,1)} %gather_keys.1.k.v, bf16[8,256,1536]{2,1,0:T(8,128)(2,1)} %get-tuple-element.66.p, ...), custom_call_target="tpu_custom_call" | custom-call | tf_op jit(solution)/shard_map/attend_back/pallas_call | solution.py:679
  267.1 22.2 %keys_home.1.dkv = f32[256,1024]{1,0:T(8,128)} custom-call(bf16[4,256,512]{2,1,0:T(8,128)(2,1)} %get-tuple-element.69.dk, bf16[4,256,512]{2,1,0:T(8,128)(2,1)} %get-tuple-element.70.dv), custom_call_target="tpu_custom_call" | custom-call | tf_op jit(solution)/shard_map/keys_home/pallas_call | solution.py:713
  289.3 8.3 %project_back.1 = (f32[256,1024]{1,0:T(8,128)}, bf16[8,8,2,128,128]{4,3,2,1,0:T(8,128)(2,1)}, f32[1,1024]{1,0:T(1,128)}) custom-call(f32[256,1024]{1,0:T(8,128)} %get-tuple-element.68.dq, f32[256,1024]{1,0:T(8,128)} %keys_home.1.dkv, bf16[256,1024]{1,0:T(8,128)(2,1)} %get-tuple-element.51.x, bf16[256,1024]{1,0:T(8,128)(2,1)} %get-tuple-element.71.act, ...), custom_call_target="tpu_custom_call" | custom-call | tf_op jit(solution)/shard_map/project_back/pallas_call | solution.py:754
  298.9 111.3 %reduce_all.1 = (bf16[8,12,128,128]{3,2,1,0:T(8,128)(2,1)}, f32[8,1024]{1,0:T(8,128)}, bf16[2,128,1024]{2,1,0:T(8,128)(2,1)}, f32[2,128,1024]{2,1,0:T(8,128)}) custom-call(bf16[8,9,128,128]{3,2,1,0:T(8,128)(2,1)} %get-tuple-element.62.grads, bf16[8,8,1,128,128]{4,3,2,1,0:T(8,128)(2,1)} %get-tuple-element.65.og, ...), custom_call_target="tpu_custom_call" | custom-call | tf_op jit(solution)/shard_map/reduce_all/pallas_call | solution.py:880
  411.5 4.0 fusion.22
  415.5 3.0 copy.102
  418.5 2.7 copy.103
  421.3 3.0 copy.104
  427.0 3.5 copy.101
  430.5 3.5 copy.106
  434.1 6.9 %multiply_subtract_fusion = (f32[6,128,1024]{1,2,0:T(8,128)}, f32[6,128,1024]{1,2,0:T(8,128)}, f32[6,128,1024]{1,2,0:T(8,128)}) fusion(f32[6,128,1024]{1,2,0:T(8,128)S(1)} %copy.84, f32[6,128,512]{1,2,0:T(8,128)} %bitcast.66, f32[6,128,512]{1,2,0:T(8,128)} %bitcast.65, f32[6,128,1024]{1,2,0:T(8,128)} %copy.106, f32[6,128,1024]{1,2,0:T(8,128)} %copy.101), kind=kLoop, calls=%fused_computation.3 | loop fusion | flops 12582912 | bytes 22020096 | tf_op jit(solution)/shard_map/sub | solution.py:931
  441.0 3.7 copy.116
  447.1 3.7 copy.118
  461.0 4.1 multiply_subtract_fusion.2
  473.5 4.6 multiply_subtract_fusion.1
  (95 shorter events, 53.1 us)
Async XLA Ops:
  2.9 5.9 %copy-start.12 = (f32[128,6]{0,1:T(8,128)S(1)}, f32[128,6]{0,1:T(8,128)}, u32[]{:S(2)}) copy-start(f32[128,6]{0,1:T(8,128)} %param.30) | copy-start | bytes 9220
  2.9 6.0 %copy-start.17 = (f32[2,128]{1,0:T(2,128)S(1)}, f32[2,128]{1,0:T(2,128)}, u32[]{:S(2)}) copy-start(f32[2,128]{1,0:T(2,128)} %param.31) | copy-start | bytes 3076
  2.9 10.2 %copy-start.16 = (s32[2,128,2]{1,2,0:T(2,128)S(1)}, s32[2,128,2]{1,2,0:T(2,128)}, u32[]{:S(2)}) copy-start(s32[2,128,2]{1,2,0:T(2,128)} %param.24) | copy-start | bytes 6148
  96.8 26.5 %copy-start.15 = (s32[2,1024]{1,0:T(2,128)S(1)}, s32[2,1024]{1,0:T(2,128)}, u32[]{:S(2)}) copy-start(s32[2,1024]{1,0:T(2,128)} %param.23) | copy-start | bytes 24580
  289.3 8.3 %copy-start.11 = (f32[8,1024]{1,0:T(8,128)S(1)}, f32[8,1024]{1,0:T(8,128)}, u32[]{:S(2)}) copy-start(f32[8,1024]{1,0:T(8,128)} %get-tuple-element.74) | copy-start | bytes 98308
  298.9 112.1 %copy-start.18 = (f32[2,128]{1,0:T(2,128)S(1)}, f32[2,128]{1,0:T(2,128)}, u32[]{:S(2)}) copy-start(f32[2,128]{1,0:T(2,128)} %param.43) | copy-start | bytes 3076
  298.9 112.1 %copy-start.19 = (f32[2,128]{1,0:T(2,128)S(1)}, f32[2,128]{1,0:T(2,128)}, u32[]{:S(2)}) copy-start(f32[2,128]{1,0:T(2,128)} %param.42) | copy-start | bytes 3076
  441.0 3.7 copy-start.1
  447.1 3.7 copy-start
  451.6 2.6 copy-start.2
  454.3 5.4 %copy-start.5 = (f32[128,2048]{1,0:T(8,128)S(1)}, f32[128,2048]{1,0:T(8,128)}, u32[]{:S(2)}) copy-start(f32[128,2048]{1,0:T(8,128)} %param.26) | copy-start | bytes 3145732
  465.1 6.5 %copy-start.3 = (f32[8,3,128,128]{3,2,1,0:T(8,128)S(1)}, f32[8,3,128,128]{3,2,1,0:T(8,128)}, u32[]{:S(2)}) copy-start(f32[8,3,128,128]{3,2,1,0:T(8,128)} %get-tuple-element.140) | copy-start | bytes 4718596
  471.6 1.4 copy-start.4
  471.6 1.9 copy-start.6
  473.5 5.9 %copy-start.8 = (f32[128,1024]{1,0:T(8,128)S(1)}, f32[128,1024]{1,0:T(8,128)}, u32[]{:S(2)}) copy-start(f32[128,1024]{1,0:T(8,128)} %param.27) | copy-start | bytes 1572868
  478.0 1.6 copy-start.9
  481.8 4.5 copy-start.13
  481.8 4.5 copy-start.14
  483.3 3.6 copy-start.10
  483.4 4.4 copy-start.7

commit v2 on v1

--- a/solution.py
+++ b/solution.py
@@ -932,6 +932,73 @@
     return [moment_new, square_new, updated]
 
 
+def update_kernel(*refs):
+    grads, ins, outs = refs[0], refs[1:13], refs[13:]
+    step = pl.program_id(0)
+    rates = learning_rates()
+    lane = lax.broadcasted_iota(jnp.int32, (128, 128), 1)
+
+    def apply(n, at, grad, rate):
+        m, v, w = adamw(ins[3 * n][at], grad, ins[3 * n + 1][at], ins[3 * n + 2][at], rate, 0.1)
+        outs[3 * n][at], outs[3 * n + 1][at], outs[3 * n + 2][at] = m, v, w
+
+    for b in range(3):
+
+        @pl.when(step == b)
+        def _():
+            for part in range(2):
+                for t in range(4):
+                    one = grads[2 * t, 3 * part + b].astype(f32)
+                    two = grads[2 * t + 1, 3 * part + b].astype(f32)
+                    cols = slice(FF * part + 128 * t, FF * part + 128 * t + 128)
+                    first = jnp.where(lane < SLICE, one, pltpu.roll(two, SLICE, 1))
+                    second = jnp.where(lane < SLICE, pltpu.roll(one, SLICE, 1), two)
+                    apply(0, (0, slice(None), cols), first, rates[2])
+                    apply(0, (1, slice(None), cols), second, rates[2])
+
+        @pl.when(step == 3 + b)
+        def _():
+            for k in range(8):
+                grad = grads[k, 6 + b].astype(f32)
+                for e in range(2):
+                    at = (e, slice(SLICE * k, SLICE * k + SLICE), slice(None))
+                    apply(1, at, grad[SLICE * e : SLICE * e + SLICE], rates[3])
+
+    for part in range(2):
+
+        @pl.when(step == 6 + part)
+        def _():
+            for t in range(8):
+                at = (slice(None), slice(128 * t, 128 * t + 128))
+                apply(2, at, grads[4 * part + t // 2, 10 + t % 2].astype(f32), rates[0])
+
+    @pl.when(step == 8)
+    def _():
+        for t in range(8):
+            at = (slice(None), slice(128 * t, 128 * t + 128))
+            apply(3, at, grads[t, 9].astype(f32), rates[1])
+
+
+def update(ALL, *arrays):
+    specs = [
+        pl.BlockSpec((2, 128, D), lambda i: (jnp.minimum(i, 2), 0, 0)),
+        pl.BlockSpec((2, FF, 128), lambda i: (jnp.clip(i - 3, 0, 2), 0, 0)),
+        pl.BlockSpec((128, D), lambda i: (0, jnp.clip(i - 6, 0, 1))),
+        pl.BlockSpec((128, D), lambda i: (0, 0)),
+    ]
+    dims = [(EXPERTS, 128, D), (EXPERTS, FF, 128), (128, 2 * D), (128, D)]
+    return pl.pallas_call(
+        update_kernel,
+        grid=(9,),
+        out_shape=tuple(shape(d, f32) for d in dims for _ in range(3)),
+        in_specs=[pl.BlockSpec((8, 12, 128, 128), lambda i: (0, 0, 0, 0))]
+        + [spec for spec in specs for _ in range(3)],
+        out_specs=tuple(spec for spec in specs for _ in range(3)),
+        compiler_params=params(),
+        name="update",
+    )(ALL, *arrays)
+
+
 def on_device(
     tokens, segments, routes, cotangent, w_qkv, w_out, w_gateup, w_down, w_router, w_gains,
     qkv_first, qkv_second, out_first, out_second, gateup_first, gateup_second, down_first, down_second,
@@ -980,28 +1047,13 @@
     small = jnp.concatenate([small_two[:7], small_one], axis=0)
     ALL, SM, layer_out, input_grad = reduce_all(grads, og, qg, small, out, gin)
 
-    ALL = ALL.astype(f32)
-    gate_up = [
-        ALL[:, b : b + 3].reshape(8, 3, 128, 2, SLICE).transpose(1, 3, 2, 0, 4).reshape(EXPERTS, 128, FF)
-        for b in (0, 3)
-    ]
+    big = update(ALL, w_gateup, gateup_first, gateup_second, w_down, down_first, down_second,
+                 w_qkv, qkv_first, qkv_second, w_out, out_first, out_second)
     mine = cut(SM, shard * 128, 128, 1)
-    summed = (
-        ALL[:, 10:12].transpose(2, 0, 1, 3).reshape(128, 2 * D),
-        ALL[:, 9].transpose(1, 0, 2).reshape(128, D),
-        jnp.concatenate(gate_up, axis=2),
-        ALL[:, 6:9].reshape(8, EXPERTS, SLICE, 128).transpose(1, 0, 2, 3).reshape(EXPERTS, FF, 128),
-        mine[:6].T,
-        jnp.stack([mine[7], mine[6]]),
-    )
-    masters = (w_qkv, w_out, w_gateup, w_down, w_router, w_gains)
-    firsts = (qkv_first, out_first, gateup_first, down_first, router_first, gains_first)
-    seconds = (qkv_second, out_second, gateup_second, down_second, router_second, gains_second)
-    decays = (0.1, 0.1, 0.1, 0.1, 0.1, 0.0)
-    results = []
-    for n in range(6):
-        results += adamw(masters[n], summed[n], firsts[n], seconds[n], learning_rates()[n], decays[n])
-    return (layer_out, input_grad, *results)
+    rates = learning_rates()
+    router = adamw(w_router, mine[:6].T, router_first, router_second, rates[4], 0.1)
+    gains = adamw(w_gains, jnp.stack([mine[7], mine[6]]), gains_first, gains_second, rates[5], 0.0)
+    return (layer_out, input_grad, *big[6:9], *big[9:12], *big[0:3], *big[3:6], *router, *gains)
 
 
 def solution(mesh):

time: 490 us -> 435 us (0.89)
  local copies, waits for them, and re-layouts: 70.8 us -> 13.2 us
  Pallas kernels: 392 us -> 412 us
  other arithmetic: 25 us -> 8.26 us
    unnamed x60 -> x22, local copies, waits for them, and re-layouts: 43.7 us -> 2.08 us
    pallas_call x0 -> x1, Pallas kernels: none -> 19.6 us  [update(): pl.pallas_call(update_kernel, grid=(9,), out_shape=tuple((shape(d, f32) f...]
    sub x6 -> x2, other arithmetic: 18.3 us -> 1.21 us  [adamw(): updated = weight - step_rate * (corrected / spread_by + decay_rate * weight)]
    slice x3 -> x0, local copies, waits for them, and re-layouts: 10 us -> none  [the longest x2 6.04 us: on_device(): ALL[:, b:b + 3].reshape(8, 3, 128, 2, SLICE).transpose(1, 3, 2, 0, 4)]
    transpose x7 -> x0, local copies, waits for them, and re-layouts: 7.29 us -> none  [the longest x2 5.45 us: on_device(): ALL[:, b:b + 3].reshape(8, 3, 128, 2, SLICE).transpose(1, 3, 2, 0, 4)]
where the time goes in v2:
time: 435 us; the launch traced here: 434 us
  Pallas kernels  412 us (95%)
  local copies, waits for them, and re-layouts  13.2 us (3%)
  other arithmetic  8.26 us (2%)
    pallas_call x1, Pallas kernels, reduce_all(): pl.pallas_call(reduce_kernel, out_shape=(shape((8, 12, 128, 128), b16), s...  112 us
    pallas_call x1, Pallas kernels, gather(): pl.pallas_call(gather_kernel, out_shape=(shape((ROWS, D), b16), shape((RO...  82.1 us
    pallas_call x1, Pallas kernels, send_home(): pl.pallas_call(home_kernel, out_shape=shape((ROWS, wide), f32), in_specs=...  52.9 us
    pallas_call x1, Pallas kernels, gather_tokens(): pl.pallas_call(tokens_kernel, out_shape=shape((8, ROWS, D + 128), b16), i...  28.5 us
    pallas_call x1, Pallas kernels, experts(): pl.pallas_call(experts_kernel, grid=(8,), out_shape=(shape((8, ROWS, 2 *...  25.1 us
    pallas_call x1, Pallas kernels, keys_home(): pl.pallas_call(keys_home_kernel, out_shape=shape((ROWS, D), f32), in_spec...  22.2 us
    pallas_call x1, Pallas kernels, gather_keys(): pl.pallas_call(keys_kernel, out_shape=shape((4, ROWS, D), b16), in_specs=...  20.4 us
    pallas_call x1, Pallas kernels, update(): pl.pallas_call(update_kernel, grid=(9,), out_shape=tuple((shape(d, f32) f...  19.6 us

profile of v2, /device:TPU:1, one launch (start us, length us, event | category | flops | bytes accessed | tf_op | source)
XLA Modules:
  0.0 434.2 jit_solution(4331831010531916538)
XLA Ops:
  3.7 1.3 constant_dynamic-slice_fusion.1.segk
  5.0 0.9 dynamic-slice_convert_fusion.2
  8.3 1.6 dynamic-slice_convert_fusion.1.wo
  10.0 0.8 copy.59.segq
  10.8 1.8 dynamic-slice_convert_fusion.wq
  12.5 1.3 constant_dynamic-slice_fusion.3
  15.6 0.8 pad_maximum_fusion.2.sin
  16.5 0.8 pad_maximum_fusion.1.cos
  17.3 82.1 %gather.1 = (bf16[256,1024]{1,0:T(8,128)(2,1)}, f32[256,128]{1,0:T(8,128)}, bf16[8,256,1024]{2,1,0:T(8,128)(2,1)}, bf16[2,1024,1024]{2,1,0:T(8,128)(2,1)}, bf16[...) custom-call(bf16[2,128,1024]{2,1,0:T(8,128)(2,1)} %xl.1, bf16[2,128,1024]{2,1,0:T(8,128)(2,1)} %gl.1, ...), custom_call_target="tpu_custom_call" | custom-call | tf_op jit(solution)/shard_map/gather/pallas_call | solution.py:221
  99.4 4.5 %project.1 = (bf16[256,1024]{1,0:T(8,128)(2,1)}, bf16[256,1024]{1,0:T(8,128)(2,1)}, bf16[256,1024]{1,0:T(8,128)(2,1)}) custom-call(bf16[256,1024]{1,0:T(8,128)(2,1)} %get-tuple-element.63.x, bf16[2,1024,1024]{2,1,0:T(8,128)(2,1)} %get-tuple-element.64.wq, bf16[400,1024]{1,0:T(8,128)(2,1)} %get-tuple-element.65.gains.tail.dn.refs_4_, ...), custom_call_target="tpu_custom_call" | custom-call | tf_op jit(solution)/shard_map/project/pallas_call | solution.py:267
  103.9 20.4 %gather_keys.1.k.v = bf16[4,256,1024]{2,1,0:T(8,128)(2,1)} custom-call(bf16[256,1024]{1,0:T(8,128)(2,1)} %get-tuple-element.67.kv), custom_call_target="tpu_custom_call" | custom-call | tf_op jit(solution)/shard_map/gather_keys/pallas_call | solution.py:297
  124.3 11.9 %attend.1 = (bf16[256,1024]{1,0:T(8,128)(2,1)}, bf16[8,256,1536]{2,1,0:T(8,128)(2,1)}) custom-call(bf16[256,1024]{1,0:T(8,128)(2,1)} %get-tuple-element.66.q, bf16[4,256,1024]{2,1,0:T(8,128)(2,1)} %gather_keys.1.k.v, bf16[4,256,1024]{2,1,0:T(8,128)(2,1)} %gather_keys.1.k.v, s32[256,1]{1,0:T(8,128)} %copy.58.posq, s32[256,1]{1,0:T(8,128)} %copy.59.segq, ...), custom_call_target="tpu_custom_call" | custom-call | tf_op jit(solution)/shard_map/attend/pallas_call | solution.py:368
  136.2 4.2 after_attention.1
  140.4 28.5 %gather_tokens.1.act = bf16[8,256,1152]{2,1,0:T(8,128)(2,1)} custom-call(bf16[256,1152]{1,0:T(8,128)(2,1)} %get-tuple-element.71.act.refs_2_), custom_call_target="tpu_custom_call" | custom-call | tf_op jit(solution)/shard_map/gather_tokens/pallas_call | solution.py:460
  168.9 25.1 %experts.1 = (bf16[8,256,2176]{2,1,0:T(8,128)(2,1)}, bf16[8,9,128,128]{3,2,1,0:T(8,128)(2,1)}) custom-call(bf16[8,256,1152]{2,1,0:T(8,128)(2,1)} %gather_tokens.1.act, bf16[8,256,1024]{2,1,0:T(8,128)(2,1)} %get-tuple-element.72.g.refs_3_, bf16[1024,768]{1,0:T(8,128)(2,1)} %get-tuple-element.73.gu, bf16[400,1024]{1,0:T(8,128)(2,1)} %get-tuple-element.65.gains.tail.dn.refs_4_), custom_call_target="tpu_custom_call" | custom-call | tf_op jit(solution)/shard_map/experts/pallas_call | solution.py:514
  193.9 52.9 %send_home.1.refs_0_ = f32[256,2176]{1,0:T(8,128)} custom-call(bf16[8,256,2176]{2,1,0:T(8,128)(2,1)} %get-tuple-element.75.part), custom_call_target="tpu_custom_call" | custom-call | tf_op jit(solution)/shard_map/send_home/pallas_call | solution.py:557
  246.8 7.4 %middle.1 = (bf16[256,1024]{1,0:T(8,128)(2,1)}, f32[256,1024]{1,0:T(8,128)}, bf16[256,1024]{1,0:T(8,128)(2,1)}, bf16[8,8,1,128,128]{4,3,2,1,0:T(8,128)(2,1)}, f32[8,1024]{1,0:T(8,128)}) custom-call(s32[1]{0:T(128)} %bitcast.10.slot, f32[256,2176]{1,0:T(8,128)} %send_home.1.refs_0_, f32[256,1024]{1,0:T(8,128)} %get-tuple-element.76.refs_1_, ...), custom_call_target="tpu_custom_call" | custom-call | tf_op jit(solution)/shard_map/middle/pallas_call | solution.py:605
  254.3 13.2 %attend_back.1 = (f32[256,1024]{1,0:T(8,128)}, bf16[4,256,512]{2,1,0:T(8,128)(2,1)}, bf16[4,256,512]{2,1,0:T(8,128)(2,1)}) custom-call(bf16[256,1024]{1,0:T(8,128)(2,1)} %get-tuple-element.66.q, bf16[4,256,1024]{2,1,0:T(8,128)(2,1)} %gather_keys.1.k.v, bf16[4,256,1024]{2,1,0:T(8,128)(2,1)} %gather_keys.1.k.v, bf16[8,256,1536]{2,1,0:T(8,128)(2,1)} %get-tuple-element.78.p, ...), custom_call_target="tpu_custom_call" | custom-call | tf_op jit(solution)/shard_map/attend_back/pallas_call | solution.py:679
  267.4 22.2 %keys_home.1.dkv = f32[256,1024]{1,0:T(8,128)} custom-call(bf16[4,256,512]{2,1,0:T(8,128)(2,1)} %get-tuple-element.81.dk, bf16[4,256,512]{2,1,0:T(8,128)(2,1)} %get-tuple-element.82.dv), custom_call_target="tpu_custom_call" | custom-call | tf_op jit(solution)/shard_map/keys_home/pallas_call | solution.py:713
  289.6 8.3 %project_back.1 = (f32[256,1024]{1,0:T(8,128)}, bf16[8,8,2,128,128]{4,3,2,1,0:T(8,128)(2,1)}, f32[1,1024]{1,0:T(1,128)}) custom-call(f32[256,1024]{1,0:T(8,128)} %get-tuple-element.80.dq, f32[256,1024]{1,0:T(8,128)} %keys_home.1.dkv, bf16[256,1024]{1,0:T(8,128)(2,1)} %get-tuple-element.63.x, bf16[256,1024]{1,0:T(8,128)(2,1)} %get-tuple-element.83.act, ...), custom_call_target="tpu_custom_call" | custom-call | tf_op jit(solution)/shard_map/project_back/pallas_call | solution.py:754
  298.0 1.3 pad_maximum_fusion.3.small
  299.3 111.6 %reduce_all.1 = (bf16[8,12,128,128]{3,2,1,0:T(8,128)(2,1)}, f32[8,1024]{1,0:T(8,128)}, bf16[2,128,1024]{2,1,0:T(8,128)(2,1)}, f32[2,128,1024]{2,1,0:T(8,128)}) custom-call(bf16[8,9,128,128]{3,2,1,0:T(8,128)(2,1)} %get-tuple-element.74.grads, bf16[8,8,1,128,128]{4,3,2,1,0:T(8,128)(2,1)} %get-tuple-element.77.og, ...), custom_call_target="tpu_custom_call" | custom-call | tf_op jit(solution)/shard_map/reduce_all/pallas_call | solution.py:880
  412.9 19.6 %update.1 = (f32[6,128,1024]{2,1,0:T(8,128)}, f32[6,128,1024]{2,1,0:T(8,128)}, f32[6,128,1024]{2,1,0:T(8,128)}, f32[6,512,128]{2,1,0:T(8,128)}, f32[6,512,128]{2...) custom-call(bf16[8,12,128,128]{3,2,1,0:T(8,128)(2,1)} %get-tuple-ele, ...), custom_call_target="tpu_custom_call" | custom-call | tf_op jit(solution)/shard_map/update/pallas_call | solution.py:990
  433.3 1.0 copy.65
  (43 shorter events, 9.8 us)
Async XLA Ops:
  289.6 8.4 %copy-start.2 = (f32[8,1024]{1,0:T(8,128)S(1)}, f32[8,1024]{1,0:T(8,128)}, u32[]{:S(2)}) copy-start(f32[8,1024]{1,0:T(8,128)} %get-tuple-element.86) | copy-start | bytes 98308
  299.3 112.3 %copy-start.6 = (f32[2,128]{1,0:T(2,128)S(1)}, f32[2,128]{1,0:T(2,128)}, u32[]{:S(2)}) copy-start(f32[2,128]{1,0:T(2,128)} %param.31) | copy-start | bytes 3076
  299.3 112.3 %copy-start.7 = (f32[2,128]{1,0:T(2,128)S(1)}, f32[2,128]{1,0:T(2,128)}, u32[]{:S(2)}) copy-start(f32[2,128]{1,0:T(2,128)} %param.43) | copy-start | bytes 3076
  299.3 112.3 %copy-start.8 = (f32[2,128]{1,0:T(2,128)S(1)}, f32[2,128]{1,0:T(2,128)}, u32[]{:S(2)}) copy-start(f32[2,128]{1,0:T(2,128)} %param.42) | copy-start | bytes 3076
  299.3 112.9 %copy-start.3 = (f32[128,6]{0,1:T(8,128)S(1)}, f32[128,6]{0,1:T(8,128)}, u32[]{:S(2)}) copy-start(f32[128,6]{0,1:T(8,128)} %param.30) | copy-start | bytes 9220
  299.3 112.9 %copy-start.4 = (f32[128,6]{0,1:T(8,128)S(1)}, f32[128,6]{0,1:T(8,128)}, u32[]{:S(2)}) copy-start(f32[128,6]{0,1:T(8,128)} %param.41) | copy-start | bytes 9220
  299.3 112.9 %copy-start.5 = (f32[128,6]{0,1:T(8,128)S(1)}, f32[128,6]{0,1:T(8,128)}, u32[]{:S(2)}) copy-start(f32[128,6]{0,1:T(8,128)} %param.40) | copy-start | bytes 9220
  412.9 19.6 %copy-start.1 = (bf16[2,128,1024]{2,1,0:T(8,128)(2,1)S(1)}, bf16[2,128,1024]{2,1,0:T(8,128)(2,1)}, u32[]{:S(2)}) copy-start(bf16[2,128,1024]{2,1,0:T(8,128)(2,1)} %get-tuple-element.144) | copy-start | bytes 1572868
  412.9 20.4 %copy-start = (f32[2,128,1024]{2,1,0:T(8,128)S(1)}, f32[2,128,1024]{2,1,0:T(8,128)}, u32[]{:S(2)}) copy-start(f32[2,128,1024]{2,1,0:T(8,128)} %get-tuple-element.145) | copy-start | bytes 3145732
